TPU v7x, 128 devices: a whole 4x4x4 slice. The times are simulated.
128 devices in a mesh: wide: 32 (over z, x, core), narrow: 4 (over y).
Axes of the slice: x: 4, y: 4, z: 4, core: 2. Of those that a mesh axis runs over, the one named last changes fastest.
Arguments:
- features: bfloat16 [65536, 256], P(('wide', 'narrow')), may hold values from -6 to 6
- neighbours: int32 [65536, 8], P(('wide', 'narrow')), may hold values from 0 to 2047
- code_ids: int32 [65536, 16], P(('wide', 'narrow')), may hold values from 0 to 4095
- assignment: int32 [65536], P(('wide', 'narrow')), may hold values from 0 to 4095
- cotangent: bfloat16 [65536, 256], P(('wide', 'narrow')), may hold values from -6 to 6
- code_sums: float32 [4096, 256], replicated, may hold values from -24 to 24
- code_counts: float32 [4096], replicated, may hold values from 1 to 10
- self_weight: bfloat16 [256, 256], replicated, may hold values from -0.375 to 0.375
- neighbour_weight: bfloat16 [256, 256], replicated, may hold values from -0.375 to 0.375
Outputs:
- output: bfloat16 [65536, 256], P(('wide', 'narrow'))
- feature_grad: bfloat16 [65536, 256], P(('wide', 'narrow'))
- self_grad: float32 [256, 256], replicated
- neighbour_grad: float32 [256, 256], replicated
- new_codebook: float32 [4096, 256], P(('wide', 'narrow'))
- code_grad: float32 [4096, 256], P(('wide', 'narrow'))
All inputs are finite; a program needn't handle non-finite values.
Results may differ from a plain program's by a relative error of at most 0.0075.
Values may be sent and summed in bfloat16 or wider, within the bound.
A program may use at most 128 MiB of HBM per device.

v0:
```python
import math

import jax
import jax.numpy as jnp
from jax import lax
from jax.sharding import PartitionSpec as P

decay_rate = 0.5


def on_device(
    features,
    neighbours,
    code_ids,
    assignment,
    cotangent,
    code_sums,
    code_counts,
    self_weight,
    neighbour_weight,
):
    node_rows = features.shape[0]
    width = features.shape[1]
    code_total = code_sums.shape[0]
    slot_count = neighbours.shape[1]
    pick_count = code_ids.shape[1]
    block_rows = math.gcd(node_rows, 512)
    block_count = node_rows // block_rows
    codebook = (code_sums / code_counts[:, None]).astype(jnp.bfloat16)
    code_iota = lax.broadcasted_iota(jnp.int32, (1, code_total), 1)
    piece_rows = lax.all_gather(features, "narrow", axis=0, tiled=True)
    length = piece_rows.shape[0]
    relative = neighbours
    inside_mask = (relative >= 0) & (relative < length)
    taken_rows = jnp.take(piece_rows, jnp.clip(relative, 0, length - 1), axis=0)
    kept_rows = jnp.where(inside_mask[:, :, None], taken_rows.astype(jnp.float32), 0.0)
    near = jnp.sum(kept_rows, axis=1)

    def pick_table(block_ids):
        table = jnp.zeros((block_ids.shape[0], code_total), jnp.float32)
        for pick_index in range(pick_count):
            table = table + (block_ids[:, pick_index : pick_index + 1] == code_iota).astype(
                jnp.float32
            )
        return table.astype(jnp.bfloat16)

    def code_block(block_ids):
        return jnp.dot(pick_table(block_ids), codebook, preferred_element_type=jnp.float32)

    far = lax.map(code_block, code_ids.reshape(block_count, block_rows, pick_count)).reshape(
        node_rows, width
    )
    agg = (near / slot_count + far / pick_count).astype(jnp.bfloat16)

    def stat_block(carried, inputs):
        block_assign, block_feats = inputs
        table = (block_assign[:, None] == code_iota).astype(jnp.bfloat16)
        sums_part = jnp.einsum("bk,bf->kf", table, block_feats, preferred_element_type=jnp.float32)
        counts_part = jnp.sum(table.astype(jnp.float32), axis=0)
        return ((carried[0] + sums_part, carried[1] + counts_part), None)

    stat_init = (jnp.zeros((code_total, width), jnp.float32), jnp.zeros((code_total,), jnp.float32))
    (assigned_sum, assigned_count), unused_stats = lax.scan(
        stat_block,
        stat_init,
        (
            assignment.reshape(block_count, block_rows),
            features.reshape(block_count, block_rows, width),
        ),
    )
    hidden = jnp.dot(features, self_weight, preferred_element_type=jnp.float32) + jnp.dot(
        agg, neighbour_weight, preferred_element_type=jnp.float32
    )
    sigma = jax.nn.sigmoid(hidden)
    output = (hidden * sigma).astype(jnp.bfloat16)
    hidden_grad = (cotangent.astype(jnp.float32) * sigma * (1.0 + hidden * (1.0 - sigma))).astype(
        jnp.bfloat16
    )
    self_local = jnp.einsum("nf,nh->fh", features, hidden_grad, preferred_element_type=jnp.float32)
    neighbour_local = jnp.einsum("nf,nh->fh", agg, hidden_grad, preferred_element_type=jnp.float32)
    agg_grad = jnp.einsum(
        "nh,fh->nf", hidden_grad, neighbour_weight, preferred_element_type=jnp.float32
    ).astype(jnp.bfloat16)

    def grad_block(carried, inputs):
        block_ids, block_grad = inputs
        return (
            carried
            + jnp.einsum(
                "bk,bf->kf", pick_table(block_ids), block_grad, preferred_element_type=jnp.float32
            ),
            None,
        )

    code_local, unused_grad = lax.scan(
        grad_block,
        jnp.zeros((code_total, width), jnp.float32),
        (
            code_ids.reshape(block_count, block_rows, pick_count),
            agg_grad.reshape(block_count, block_rows, width),
        ),
    )
    code_local = code_local / pick_count
    spread_term = agg_grad.astype(jnp.float32) / slot_count
    term = jnp.zeros((node_rows * lax.axis_size("narrow"), width), jnp.float32)
    for slot_index in range(slot_count):
        relative = neighbours[:, slot_index]
        inside_mask = (relative >= 0) & (relative < node_rows * lax.axis_size("narrow"))
        term = term.at[jnp.clip(relative, 0, node_rows * lax.axis_size("narrow") - 1)].add(
            jnp.where(inside_mask[:, None], spread_term, 0.0)
        )
    returned = lax.psum_scatter(
        term.astype(jnp.bfloat16), "narrow", scatter_dimension=0, tiled=True
    ).astype(jnp.float32)
    feature_grad = (
        jnp.einsum("nh,fh->nf", hidden_grad, self_weight, preferred_element_type=jnp.float32)
        + returned
    ).astype(jnp.bfloat16)
    shard_rows = code_total // lax.axis_size(("wide", "narrow"))
    shard_start = lax.axis_index(("wide", "narrow")) * shard_rows
    total_sums, total_counts, total_grad = lax.psum(
        (assigned_sum, assigned_count, code_local), ("wide", "narrow")
    )
    own_sums = lax.dynamic_slice_in_dim(total_sums, shard_start, shard_rows, 0)
    own_counts = lax.dynamic_slice_in_dim(total_counts, shard_start, shard_rows, 0)
    own_grad = lax.dynamic_slice_in_dim(total_grad, shard_start, shard_rows, 0)
    old_sums = lax.dynamic_slice_in_dim(code_sums, shard_start, shard_rows, 0)
    old_counts = lax.dynamic_slice_in_dim(code_counts, shard_start, shard_rows, 0)
    new_codebook = (decay_rate * old_sums + (1.0 - decay_rate) * own_sums) / (
        decay_rate * old_counts + (1.0 - decay_rate) * own_counts
    )[:, None]
    self_grad, neighbour_grad = lax.psum((self_local, neighbour_local), ("wide", "narrow"))
    return (output, feature_grad, self_grad, neighbour_grad, new_codebook, own_grad)


def solution(mesh):
    return jax.shard_map(
        on_device,
        mesh=mesh,
        in_specs=(
            P(("wide", "narrow"), None),
            P(("wide", "narrow"), None),
            P(("wide", "narrow"), None),
            P(("wide", "narrow")),
            P(("wide", "narrow"), None),
            P(),
            P(),
            P(),
            P(),
        ),
        out_specs=(
            P(("wide", "narrow"), None),
            P(("wide", "narrow"), None),
            P(),
            P(),
            P(("wide", "narrow"), None),
            P(("wide", "narrow"), None),
        ),
        check_vma=False,
    )
```

profile of v0, /device:TPU:1, one launch (start us, length us, event | category | flops | bytes accessed | tf_op | source)
XLA Modules:
  0.0 319.3 jit_solution(4325635187871313165)
XLA Ops:
  8.7 0.7 compare_and_fusion.1
  9.4 1.1 compare_select_fusion.1
  10.5 1.1 and_reduce_fusion
  11.6 1.2 fusion.50
  13.4 1.1 fusion.49
  14.5 5.6 %fusion.1 = f32[4096,256]{1,0:T(8,128)} fusion(bf16[512,256]{1,0:T(8,128)(2,1)} %param.9, s32[512]{0:T(512)} %param.12), kind=kOutput, calls=%fused_computation.12 | convolution fusion | flops 1075838976 | bytes 4458496 | tf_op jit(solution)/shard_map/while/body/eval_jaxpr/bk,bf->kf/dot_general | solution.py:58
  20.1 1.7 divide_convert_fusion.11
  21.8 14.2 %all-gather.2.cloned.1.call-done = bf16[2048,256]{1,0:T(8,128)(2,1)} async-done(((bf16[512,256]{1,0:T(8,128)(2,1)}), bf16[2048,256]{1,0:T(8,128)(2,1)}) %all-gather.2.cloned.1.call-update) | async-done | bytes 1048592 | tf_op jit(solution)/shard_map/all_gather | solution.py:31
  36.0 14.3 %gather_fusion = bf16[4096,256]{1,0:T(8,128)(2,1)S(1)} fusion(bf16[2048,256]{1,0:T(8,128)(2,1)} %all-gather.2.cloned.1.call-done, s32[4096]{0:T(1024)S(1)} %broadcast_clamp_fusion), kind=kCustom, calls=%fused_computation | custom fusion | bytes 4210688 | tf_op jit(solution)/shard_map/jit(_take)/gather | solution.py:35
  50.4 3.4 %select_reduce_fusion = f32[512,256]{1,0:T(8,128)S(1)} fusion(bf16[4096,256]{1,0:T(8,128)(2,1)S(1)} %gather_fusion, pred[512,8]{1,0:T(8,128)(4,1)S(1)} %copy.23, pred[512,8]{1,0:T(8,128)(4,1)S(1)} %copy.22), kind=kLoop, calls=%fused_computation.33 | loop fusion | flops 4063232 | bytes 2629632 | tf_op jit(solution)/shard_map/reduce_sum | solution.py:37
  53.8 19.0 %fusion.6 = bf16[512,256]{1,0:T(8,128)(2,1)S(1)} fusion(f32[512,256]{1,0:T(8,128)S(1)} %select_reduce_fusion, s32[512]{0:T(512)S(1)} %bitcast.74, s32[512]{0:T(512)S(1)} %bitcast.76, s32[512]{0:T(512)S(1)} %bitcast.48, s32[512]{0:T(512)S(1)} %bitcast.50, s32[512]{0:T(512)S(1)} %bitcast.52, s32[512]{0:T(512)S(1)} %bitcast.54, s32[512]{0:T(512)S(1)} %bitcast.56, ...), kind=kOutput, calls=%fused_computation.40 | convolution fusion | flops 1174929408 | bytes 2916352 | tf_op jit(solution)/shard_map/while/body/eval_jaxpr/dot_general | solution.py:48
  72.8 1.1 multiply_convert_fusion
  74.2 1.0 convolution_bitcast_fusion
  75.2 3.9 %scatter_custom_fusion = f32[2048,256]{1,0:T(8,128)S(1)} fusion(s32[512]{0:T(512)S(1)} %bitcast.84, f32[]{:T(128)} %constant.36.clone.1, bf16[512,256]{1,0:T(8,128)(2,1)S(1)} %convolution_convert_fusion, f32[]{:T(128)} %constant.38.clone.1, pred[512]{0:T(512)(128)(4,1)S(1)} %get-tuple-element.73), kind=kCustom, calls=%fused_computation.44 | custom fusion | flops 524288 | bytes 2361344 | tf_op jit(solution)/shard_map/scatter-add | solution.py:109
  79.1 4.2 %scatter_custom_fusion.1 = f32[2048,256]{1,0:T(8,128)S(1)} fusion(f32[2048,256]{1,0:T(8,128)S(1)} %scatter_custom_fusion, s32[512]{0:T(512)S(1)} %bitcast.83, bf16[512,256]{1,0:T(8,128)(2,1)S(1)} %convolution_convert_fusion, f32[]{:T(128)} %constant.36.clone.1, f32[]{:T(128)} %constant.38.clone.1, pred[512]{0:T(512)(128)(4,1)S(1)} %get-tuple-element.74), kind=kCustom, calls=%fused_computation.58 | custom fusion | flops 524288 | bytes 2359816 | tf_op jit(solution)/shard_map/scatter-add | solution.py:109
  83.3 4.6 %scatter_custom_fusion.2 = f32[2048,256]{1,0:T(8,128)S(1)} fusion(f32[2048,256]{1,0:T(8,128)S(1)} %scatter_custom_fusion.1, s32[512]{0:T(512)S(1)} %bitcast.82, bf16[512,256]{1,0:T(8,128)(2,1)S(1)} %convolution_convert_fusion, f32[]{:T(128)} %constant.36.clone.1, f32[]{:T(128)} %constant.38.clone.1, pred[512]{0:T(512)(128)(4,1)S(1)} %get-tuple-element.75), kind=kCustom, calls=%fused_computation.56 | custom fusion | flops 524288 | bytes 2359816 | tf_op jit(solution)/shard_map/scatter-add | solution.py:109
  88.0 4.2 %scatter_custom_fusion.3 = f32[2048,256]{1,0:T(8,128)S(1)} fusion(f32[2048,256]{1,0:T(8,128)S(1)} %scatter_custom_fusion.2, s32[512]{0:T(512)S(1)} %bitcast.81, bf16[512,256]{1,0:T(8,128)(2,1)S(1)} %convolution_convert_fusion, f32[]{:T(128)} %constant.36.clone.1, f32[]{:T(128)} %constant.38.clone.1, pred[512]{0:T(512)(128)(4,1)S(1)} %get-tuple-element.76), kind=kCustom, calls=%fused_computation.54 | custom fusion | flops 524288 | bytes 2359816 | tf_op jit(solution)/shard_map/scatter-add | solution.py:109
  92.2 4.2 %scatter_custom_fusion.4 = f32[2048,256]{1,0:T(8,128)S(1)} fusion(f32[2048,256]{1,0:T(8,128)S(1)} %scatter_custom_fusion.3, s32[512]{0:T(512)S(1)} %bitcast.80, bf16[512,256]{1,0:T(8,128)(2,1)S(1)} %convolution_convert_fusion, f32[]{:T(128)} %constant.36.clone.1, f32[]{:T(128)} %constant.38.clone.1, pred[512]{0:T(512)(128)(4,1)S(1)} %get-tuple-element.77), kind=kCustom, calls=%fused_computation.52 | custom fusion | flops 524288 | bytes 2359816 | tf_op jit(solution)/shard_map/scatter-add | solution.py:109
  96.5 4.2 %scatter_custom_fusion.5 = f32[2048,256]{1,0:T(8,128)S(1)} fusion(f32[2048,256]{1,0:T(8,128)S(1)} %scatter_custom_fusion.4, s32[512]{0:T(512)S(1)} %bitcast.79, bf16[512,256]{1,0:T(8,128)(2,1)S(1)} %convolution_convert_fusion, f32[]{:T(128)} %constant.36.clone.1, f32[]{:T(128)} %constant.38.clone.1, pred[512]{0:T(512)(128)(4,1)S(1)} %get-tuple-element.78), kind=kCustom, calls=%fused_computation.50 | custom fusion | flops 524288 | bytes 2359816 | tf_op jit(solution)/shard_map/scatter-add | solution.py:109
  100.7 4.2 %scatter_custom_fusion.6 = f32[2048,256]{1,0:T(8,128)S(1)} fusion(f32[2048,256]{1,0:T(8,128)S(1)} %scatter_custom_fusion.5, s32[512]{0:T(512)S(1)} %bitcast.78, bf16[512,256]{1,0:T(8,128)(2,1)S(1)} %convolution_convert_fusion, f32[]{:T(128)} %constant.36.clone.1, f32[]{:T(128)} %constant.38.clone.1, pred[512]{0:T(512)(128)(4,1)S(1)} %get-tuple-element.79), kind=kCustom, calls=%fused_computation.48 | custom fusion | flops 524288 | bytes 2359816 | tf_op jit(solution)/shard_map/scatter-add | solution.py:109
  104.9 4.2 %scatter_custom_fusion.7 = f32[2048,256]{1,0:T(8,128)S(1)} fusion(f32[2048,256]{1,0:T(8,128)S(1)} %scatter_custom_fusion.6, s32[512]{0:T(512)S(1)} %bitcast.45, bf16[512,256]{1,0:T(8,128)(2,1)S(1)} %convolution_convert_fusion, f32[]{:T(128)} %constant.36.clone.1, f32[]{:T(128)} %constant.38.clone.1, pred[512]{0:T(512)(128)(4,1)S(1)} %get-tuple-element.72), kind=kCustom, calls=%fused_computation.46 | custom fusion | flops 524288 | bytes 2359816 | tf_op jit(solution)/shard_map/scatter-add | solution.py:109
  109.2 1.1 convert_element_type.168
  110.5 1.0 fusion.51
  111.5 19.7 %convolution_multiply_fusion = f32[4096,256]{1,0:T(8,128)} fusion(bf16[512,256]{1,0:T(8,128)(2,1)S(1)} %convolution_convert_fusion, s32[512]{0:T(512)S(1)} %bitcast.75, s32[512]{0:T(512)S(1)} %bitcast.77, s32[512]{0:T(512)S(1)} %bitcast.49, s32[512]{0:T(512)S(1)} %bitcast.51, s32[512]{0:T(512)S(1)} %bitcast.53, s32[512]{0:T(512)S(1)} %bitcast.55, ...), kind=kOutput, calls=%fused_computation.30 | convolution fusion | flops 1175453696 | bytes 4489216 | tf_op jit(solution)/shard_map/while/body/eval_jaxpr/bk,bf->kf/dot_general | solution.py:89
  131.9 2.0 convert_reduce_fusion
  133.9 66.2 %psum.38 = f32[4096]{0:T(1024)S(1)} all-reduce(f32[4096]{0:T(1024)S(1)} %convert_reduce_fusion), channel_id=1, replica_groups=mesh['wide'=32,'narrow'=4] {'wide','narrow'}, use_global_device_ids=true, to_apply=%region_14.15 | all-reduce | flops 4096 | bytes 32768 | tf_op jit(solution)/shard_map/psum | solution.py:121
  200.1 1.9 fusion.7
  202.1 104.1 %all-reduce.3.cloned.1.call-done = (f32[256,256]{0,1:T(8,128)}, f32[256,256]{1,0:T(8,128)}, f32[4096,256]{1,0:T(8,128)}, f32[4096,256]{1,0:T(8,128)}) async-done(((f32[256,256]{0,1:T(8,128)}, f32[256,256]{1,0:T(8,128)}, f32[4096,256]{1,0:T(8,128)}, f32[4096,256]{1,0:T(8,128)}), (f32[256,256]{0,1:T(8,128)}, f32[256,256]{1,0:T(8,128)}, f32[4096,256]{1,0:T(8,128)}, ...) | async-done | bytes 8912912 | tf_op jit(solution)/shard_map/psum | solution.py:132
  306.2 1.8 copy.25
  308.0 1.4 constant_dynamic-slice_fusion
  309.4 1.5 multiply_divide_fusion
  310.8 1.7 copy.37
  (29 shorter events, 3.4 us)
Async XLA Ops:
  7.2 65.6 %copy-start = (bf16[256,256]{1,0:T(8,128)(2,1)S(1)}, bf16[256,256]{1,0:T(8,128)(2,1)}, u32[]{:S(2)}) copy-start(bf16[256,256]{1,0:T(8,128)(2,1)} %param.17) | copy-start | bytes 393220
  7.2 28.8 %all-gather.2.cloned.1.call-start = ((), (), s32[]{:S(2)}) async-start(), calls=%async_computation.1 | async-start | bytes 1310720 | tf_op jit(solution)/shard_map/all_gather | solution.py:31
  7.9 192.2 %reduce-scatter.2.cloned.1.call-start = ((), (), s32[]{:S(2)}) async-start(), calls=%async_computation.2 | async-start | bytes 1310720 | tf_op jit(solution)/shard_map/reduce_scatter | solution.py:112
  13.2 6.9 %copy-start.4 = (f32[4096]{0:T(1024)S(1)}, f32[4096]{0:T(1024)}, u32[]{:S(2)}) copy-start(f32[4096]{0:T(1024)} %param.15) | copy-start | bytes 49156
  13.4 6.7 %copy-start.1 = (f32[4096,256]{1,0:T(8,128)S(1)}, f32[4096,256]{1,0:T(8,128)}, u32[]{:S(2)}) copy-start(f32[4096,256]{1,0:T(8,128)} %param.14) | copy-start | bytes 12582916
  53.8 19.0 %copy-start.5 = (bf16[512,256]{1,0:T(8,128)(2,1)S(1)}, bf16[512,256]{1,0:T(8,128)(2,1)}, u32[]{:S(2)}) copy-start(bf16[512,256]{1,0:T(8,128)(2,1)} %param.13) | copy-start | bytes 786436
  72.8 1.4 copy-start.2
  110.3 195.9 %all-reduce.3.cloned.1.call-start = ((), (), s32[]{:S(2)}) async-start(), calls=%async_computation.3 | async-start | bytes 17825792 | tf_op jit(solution)/shard_map/psum | solution.py:132
  131.2 0.7 copy-start.6
  131.2 68.9 %copy-start.3 = (bf16[256,256]{1,0:T(8,128)(2,1)S(1)}, bf16[256,256]{1,0:T(8,128)(2,1)}, u32[]{:S(2)}) copy-start(bf16[256,256]{1,0:T(8,128)(2,1)} %param.16) | copy-start | bytes 393220
Sparse Core Ops, SparseCore 0:
  9.7 26.2 all-gather.1
  110.4 23.3 reduce-scatter.1
  141.0 165.1 all-reduce.2
where the time goes:
time: 324 us; the launch traced here: 319 us
  waiting for transfers between devices  119 us (37%)
  blocking collectives  66.2 us (20%)
  matrix products  50.7 us (16%)
  other arithmetic  47.3 us (15%)
  local copies, waits for them, and re-layouts  21.6 us (7%)
  between operations  14.2 us (4%)
    psum x1, waiting for transfers between devices, on_device(): lax.psum((self_local, neighbour_local), ('wide', 'narrow'))  104 us
    psum x1, blocking collectives, on_device(): lax.psum((assigned_sum, assigned_count, code_local), ('wide', 'narrow'))  66.2 us
    scatter-add x8, other arithmetic, on_device(): term.at[jnp.clip(relative, 0, node_rows * lax.axis_size('narrow') - 1)]  33.9 us
    dot_general x1, matrix products, grad_block(): jnp.einsum('bk,bf->kf', pick_table(block_ids), block_grad, preferred_elem...  19.7 us
    dot_general x1, matrix products, code_block(): jnp.dot(pick_table(block_ids), codebook, preferred_element_type=jnp.float32)  19 us
    gather x1, local copies, waits for them, and re-layouts, on_device(): taken_rows = jnp.take(piece_rows, jnp.clip(relative, 0, length - 1), axis=0)  14.3 us
    all_gather x1, waiting for transfers between devices, on_device(): piece_rows = lax.all_gather(features, 'narrow', axis=0, tiled=True)  14.2 us
  transfers between devices with their start and end apart: 3, of which 2 were waited for; matrix products, arithmetic and copies ran while one was open for 12% of the time, Pallas kernels for 0%

commit v1 on v0

v1 whole, which is shorter than its diff:
```python
import functools

import jax
import jax.numpy as jnp
from jax import lax
from jax.experimental import pallas as pl
from jax.experimental.pallas import tpu as pltpu
from jax.sharding import PartitionSpec as P

MESH = pl.DeviceIdType.MESH
F32, BF16, I32 = jnp.float32, jnp.bfloat16, jnp.int32
decay_rate = 0.5
IDX_ROWS = 32
NIBBLES = 0x0F0F0F0F


def dot(a, b):
    return jnp.dot(a, b, preferred_element_type=F32)


def dot_nt(a, b):
    return lax.dot_general(a, b, (((1,), (1,)), ((), ())), preferred_element_type=F32)


def dot_tn(a, b):
    return lax.dot_general(a, b, (((0,), (0,)), ((), ())), preferred_element_type=F32)


def words_of(spots, his, vals):
    word = None
    for hi, val in zip(his, vals):
        term = jnp.where(spots == hi, val, 0)
        word = term if word is None else word + term
    return word


def fields_of(words):
    even = odd = None
    for word in words:
        low, high = word & NIBBLES, (word >> 4) & NIBBLES
        even = low if even is None else even + low
        odd = high if odd is None else odd + high
    out = []
    for field in range(8):
        part = (even, odd)[field % 2]
        shift = 8 * (field // 2)
        if shift:
            part = part >> shift
        if shift < 24:
            part = part & 255
        out.append(part.astype(F32).astype(BF16))
    return out


def kernel(
    wide, narrow, shard,
    feat, nb_t, code_t, assign, cot, sums_hbm, counts, ws, wn,
    out, fgrad, sgrad, ngrad, newcb, cgrad,
    sums, codebook, featg, daggg, idxg, ids_nt, idx_pad, tab_far, tab_near, tab_code, tab_ret, tab_asn,
    hi_t, val_t, hi_r, val_r, row_a, far, near, hid, dz_all, agg_all, acc, ret,
    wg_f, wg_tx, wg_rx, wgb_tx, wgb_rx, wgc, wgd, as_f, as_cnt, as_tx, as_rx, asb_tx, asb_rx,
    cg_tx, cg_rx, cgb_tx, cgb_rx, cnt_col,
    sums_sem, f_s, f_r, d_s, d_r, i_s, i_r, wa_s, wa_r, wb_s, wb_r, wc_s, wc_r, wd_s, wd_r,
    aa_s, aa_r, ab_s, ab_r, ca_s, ca_r, cb_s, cb_r,
):
    n = feat.shape[0]
    half = n // 2
    chips = wide // 2
    codes = sums.shape[0]
    mine = codes // narrow
    own_half = mine // 2
    grp = n * narrow
    w = lax.axis_index("wide")
    y = lax.axis_index("narrow")
    core = w % 2
    chip = w // 2
    y_right, y_left, y_far = (y + 1) % narrow, (y + 3) % narrow, (y + 2) % narrow
    other = chip * 2 + (1 - core)

    def chip_dev(step):
        return ((chip + step) % chips) * 2 + core

    def rcopy(src, dst, ssem, rsem, dev):
        return pltpu.make_async_remote_copy(
            src_ref=src, dst_ref=dst, send_sem=ssem, recv_sem=rsem, device_id=dev, device_id_type=MESH
        )

    sums_copy = pltpu.make_async_copy(sums_hbm, sums, sums_sem)
    sums_copy.start()

    barrier = pltpu.get_barrier_semaphore()
    for peer in (y_right, y_left, y_far):
        pl.semaphore_signal(barrier, inc=1, device_id=(w, peer), device_id_type=MESH)

    def greet(step, carry):
        pl.semaphore_signal(barrier, inc=1, device_id=((w + step) % wide, y), device_id_type=MESH)
        return carry

    lax.fori_loop(1, wide, greet, 0)

    featg[pl.ds(0, n), :] = feat[...]
    idxg[0, 0:8, :] = nb_t[...]
    idxg[0, 8:24, :] = code_t[...]
    idxg[0, 24:32, :] = jnp.broadcast_to(assign[...], (8, n))
    idx_pad[...] = jnp.zeros_like(idx_pad)
    nb_own = nb_t[...]
    node_bits = n.bit_length() - 1
    slot_of = ((nb_own >> node_bits) - y) & (narrow - 1)
    idx_pad[0:8, :] = (slot_of << node_bits) | (nb_own & (n - 1))
    idx_pad[8:24, :] = code_t[...]
    ids_nt[...] = jnp.transpose(idx_pad[...])

    pl.semaphore_wait(barrier, narrow - 1 + wide - 1)

    def low(slot):
        return pl.ds(slot * n, half)

    def high(slot):
        return pl.ds(slot * n + half, half)

    def gather_copies(buf, ssem, rsem):
        right, left = (w, y_right), (w, y_left)

        def make(src, dst, at, dev):
            return rcopy(buf.at[src, :], buf.at[dst, :], ssem.at[at], rsem.at[at], dev)

        return (
            make(low(0), low(3), 0, right),
            make(high(0), high(1), 1, left),
            make(high(0), high(3), 2, right),
            make(low(0), low(1), 3, left),
            make(low(3), low(2), 4, right),
            make(high(1), high(2), 5, left),
        )

    def arrived(buf, ssem, rsem, at):
        region = (low(3), high(1), high(3), low(1), low(2), high(2))[at]
        rcopy(buf.at[region, :], buf.at[region, :], ssem.at[at], rsem.at[at], (w, y_right)).wait_recv()

    f_copies = gather_copies(featg, f_s, f_r)
    for at in range(4):
        f_copies[at].start()
    i_copies = []
    for at, (peer, slot) in enumerate(((y_right, 3), (y_left, 1), (y_far, 2))):
        i_copies.append(rcopy(idxg.at[0], idxg.at[slot], i_s.at[at], i_r.at[at], (w, peer)))
        i_copies[-1].start()

    far_spots = codes // 8
    far_bits = far_spots.bit_length() - 1
    near_spots = grp // 8
    near_bits = near_spots.bit_length() - 1

    def far_tile(tile, carry):
        rows = pl.ds(pl.multiple_of(tile * 16, 16), 16)
        ids = ids_nt[rows, :]
        hi = ids & (far_spots - 1)
        val = jnp.int32(1) << ((ids >> far_bits) * 4)
        his = [jnp.broadcast_to(hi[:, 8 + j : 9 + j], (16, 128)) for j in range(16)]
        vals = [jnp.broadcast_to(val[:, 8 + j : 9 + j], (16, 128)) for j in range(16)]
        for part in range(far_spots // 128):
            spots = lax.broadcasted_iota(I32, (16, 128), 1) + part * 128
            words = (words_of(spots, his[:8], vals[:8]), words_of(spots, his[8:], vals[8:]))
            for field, counts_part in enumerate(fields_of(words)):
                tab_far[rows, pl.ds(field * far_spots + part * 128, 128)] = counts_part
        return carry

    def near_tile(tile, carry):
        rows = pl.ds(pl.multiple_of(tile * 16, 16), 16)
        ids = ids_nt[rows, :]
        hi = ids & (near_spots - 1)
        val = jnp.int32(1) << ((ids >> near_bits) * 4)
        his = [jnp.broadcast_to(hi[:, j : j + 1], (16, 128)) for j in range(8)]
        vals = [jnp.broadcast_to(val[:, j : j + 1], (16, 128)) for j in range(8)]
        for part in range(near_spots // 128):
            spots = lax.broadcasted_iota(I32, (16, 128), 1) + part * 128
            words = (words_of(spots, his, vals),)
            for field, counts_part in enumerate(fields_of(words)):
                tab_near[rows, pl.ds(field * near_spots + part * 128, 128)] = counts_part
        return carry

    def book_block(block, carry):
        rows = pl.ds(pl.multiple_of(block * 128, 128), 128)
        inverse = 1.0 / counts[pl.ds(block, 1), :]
        column = jnp.transpose(jnp.broadcast_to(inverse, (128, 128)))
        for part in range(sums.shape[1] // 128):
            lanes = pl.ds(part * 128, 128)
            codebook[rows, lanes] = (sums[rows, lanes] * column).astype(BF16)
        return carry

    lax.fori_loop(0, n // 32, far_tile, 0)
    arrived(featg, f_s, f_r, 0)
    f_copies[4].start()
    arrived(featg, f_s, f_r, 1)
    f_copies[5].start()
    lax.fori_loop(n // 32, n // 16, far_tile, 0)
    sums_copy.wait()
    lax.fori_loop(0, codes // 128, book_block, 0)
    far[...] = dot(tab_far[...], codebook[...]) * (1.0 / 16)
    lax.fori_loop(0, n // 16, near_tile, 0)
    hid[...] = dot(feat[...], ws[...])
    near[...] = dot(tab_near[:, 0:n], feat[...])
    arrived(featg, f_s, f_r, 2)
    near[...] += dot(tab_near[:, 3 * n : 4 * n], featg[3 * n : 4 * n, :])
    arrived(featg, f_s, f_r, 3)
    near[...] += dot(tab_near[:, n : 2 * n], featg[n : 2 * n, :])
    arrived(featg, f_s, f_r, 4)
    arrived(featg, f_s, f_r, 5)

    d_copies = gather_copies(daggg, d_s, d_r)
    for at in range(2):
        rows = pl.ds(at * half, half)
        total = near[rows, :] + dot(tab_near[rows, 2 * n : 3 * n], featg[2 * n : 3 * n, :])
        agg = (total * (1.0 / 8) + far[rows, :]).astype(BF16)
        agg_all[rows, :] = agg
        z = hid[rows, :] + dot(agg, wn[...])
        s = jax.nn.sigmoid(z)
        out[rows, :] = (z * s).astype(BF16)
        dz = (cot[rows, :].astype(F32) * s * (1.0 + z * (1.0 - s))).astype(BF16)
        dz_all[rows, :] = dz
        daggg[rows, :] = dot_nt(dz, wn[...]).astype(BF16)
        d_copies[(0, 1)[at]].start()
        d_copies[(3, 2)[at]].start()

    def weight_half(which, x):
        wg_f[which] = dot_tn(x, dz_all[...])

    weight_half(0, feat[...])
    weight_half(1, agg_all[...])
    wg_tx[...] = wg_f[1 - core].astype(BF16)
    wa = rcopy(wg_tx, wg_rx, wa_s, wa_r, (other, y))
    wa.start()

    for at in range(3):
        i_copies[at].wait_recv()
    shard_bits = shard.bit_length() - 1
    narrow_bits = narrow.bit_length() - 1
    mine_spots = mine // 8
    mine_bits = mine_spots.bit_length() - 1
    ret_spots = n // 8
    ret_bits = ret_spots.bit_length() - 1

    def place(k):
        kw = k >> (shard_bits + narrow_bits)
        row = ((((kw & 1) ^ core) * chips + (((kw >> 1) - chip) & (chips - 1))) << shard_bits) | (k & (shard - 1))
        return row, ((k >> shard_bits) & (narrow - 1)) == y

    for slot in range(narrow):
        lanes = pl.ds(slot * n, n)
        ids = idxg[slot, 0:8, :]
        hi_r[:, lanes] = ids & (ret_spots - 1)
        local = ids & (n - 1)
        val_r[:, lanes] = jnp.where((ids >> node_bits) == y, jnp.int32(1) << ((local >> ret_bits) * 4), 0)
        row, hit = place(idxg[slot, 8:24, :])
        hi_t[:, lanes] = row & (mine_spots - 1)
        val_t[:, lanes] = jnp.where(hit, jnp.int32(1) << ((row >> mine_bits) * 4), 0)
        row, hit = place(idxg[slot, 24:32, :])
        row_a[:, lanes] = jnp.where(hit, row, -1)

    def asn_tile(tile, carry):
        lanes = pl.ds(pl.multiple_of(tile * 128, 128), 128)
        row = jnp.broadcast_to(row_a[0:1, lanes], (16, 128))
        for part in range(mine // 16):
            spots = lax.broadcasted_iota(I32, (16, 128), 0) + part * 16
            tab_asn[pl.ds(part * 16, 16), lanes] = jnp.where(row == spots, 1.0, 0.0).astype(BF16)
        return carry

    def code_tile(tile, carry):
        lanes = pl.ds(pl.multiple_of(tile * 128, 128), 128)
        his = [jnp.broadcast_to(hi_t[j : j + 1, lanes], (16, 128)) for j in range(16)]
        vals = [jnp.broadcast_to(val_t[j : j + 1, lanes], (16, 128)) for j in range(16)]
        for part in range(mine_spots // 16):
            spots = lax.broadcasted_iota(I32, (16, 128), 0) + part * 16
            words = (words_of(spots, his[:8], vals[:8]), words_of(spots, his[8:], vals[8:]))
            for field, counts_part in enumerate(fields_of(words)):
                tab_code[pl.ds(field * mine_spots + part * 16, 16), lanes] = counts_part
        return carry

    def ret_tile(tile, carry):
        lanes = pl.ds(pl.multiple_of(tile * 128, 128), 128)
        his = [jnp.broadcast_to(hi_r[j : j + 1, lanes], (16, 128)) for j in range(8)]
        vals = [jnp.broadcast_to(val_r[j : j + 1, lanes], (16, 128)) for j in range(8)]
        for part in range(ret_spots // 16):
            spots = lax.broadcasted_iota(I32, (16, 128), 0) + part * 16
            words = (words_of(spots, his, vals),)
            for field, counts_part in enumerate(fields_of(words)):
                tab_ret[pl.ds(field * ret_spots + part * 16, 16), lanes] = counts_part
        return carry

    def split_count(count):
        big = jnp.floor(count * (1.0 / 256)) * 256.0
        lane = lax.broadcasted_iota(I32, count.shape, 1)
        return jnp.where(lane < 64, big, count - big).astype(BF16)

    def join_count(pair):
        pair = pair.astype(F32)
        return pair + pltpu.roll(pair, 64, 1)

    width = feat.shape[1]
    lax.fori_loop(0, grp // 128, asn_tile, 0)
    as_f[...] = dot(tab_asn[...], featg[...])
    as_cnt[...] = dot(tab_asn[...], jnp.ones((grp, 128), BF16))
    as_tx[:, 0:width] = as_f[own_half:, :].astype(BF16)
    as_tx[:, width:] = split_count(as_cnt[own_half:, :])
    aa = rcopy(as_tx, as_rx, aa_s, aa_r, (other, y))
    aa.start()

    tiles = grp // 128
    lax.fori_loop(0, tiles // 4, code_tile, 0)

    arrived(daggg, d_s, d_r, 0)
    d_copies[4].start()
    arrived(daggg, d_s, d_r, 1)
    d_copies[5].start()

    wa.wait_recv()
    wg_own = wg_f[core] + wg_rx[...].astype(F32)
    wg_f[core] = wg_own
    wgb_tx[...] = wg_own.astype(BF16)
    part_rows = wg_own.shape[0] // chips

    def wg_rows(step):
        return pl.ds(pl.multiple_of(((chip + step) % chips) * part_rows, part_rows), part_rows)

    wb = {}
    for step in range(1, chips):
        wb[step] = rcopy(
            wgb_tx.at[wg_rows(step), :], wgb_rx.at[step], wb_s.at[step], wb_r.at[step], (chip_dev(step), y)
        )
        wb[step].start()

    aa.wait_recv()
    as_f[0:own_half, :] += as_rx[:, 0:width].astype(F32)
    as_cnt[0:own_half, :] += join_count(as_rx[:, width:])
    ab = {}
    for step in range(chips):
        rows = pl.ds(step * shard, shard)
        asb_tx[step, :, 0:width] = as_f[rows, :].astype(BF16)
        asb_tx[step, :, width:] = split_count(as_cnt[rows, :])
        if step:
            ab[step] = rcopy(asb_tx.at[step], asb_rx.at[step], ab_s.at[step], ab_r.at[step], (chip_dev(step), y))
            ab[step].start()

    lax.fori_loop(tiles // 4, tiles // 2, code_tile, 0)

    for step in range(1, chips):
        wb[step].wait_recv()
    share = wg_f[core, wg_rows(0), :]
    for step in range(1, chips):
        share = share + wgb_rx[step].astype(F32)
    wgc[0] = share
    wc = []
    for at, (peer, slot) in enumerate(((y_right, 3), (y_left, 1), (y_far, 2))):
        wc.append(rcopy(wgc.at[0], wgc.at[slot], wc_s.at[at], wc_r.at[at], (w, peer)))
        wc[-1].start()

    lax.fori_loop(tiles // 2, tiles, code_tile, 0)

    for at in range(3):
        wc[at].wait_recv()

    def share_rows(dev):
        return pl.ds(pl.multiple_of((dev % 2) * wg_own.shape[0] + (dev // 2) * part_rows, part_rows), part_rows)

    wgd[share_rows(w), :] = (wgc[0] + wgc[1] + wgc[2] + wgc[3]).astype(BF16)

    def spread(step, carry):
        rcopy(
            wgd.at[share_rows(w), :], wgd.at[share_rows(w), :], wd_s.at[step], wd_r.at[step], ((w + step) % wide, y)
        ).start()
        return carry

    lax.fori_loop(1, wide, spread, 0)

    lax.fori_loop(0, tiles, ret_tile, 0)

    own_sum = as_f[0:shard, :]
    own_cnt = as_cnt[0:shard, :]
    for step in range(1, chips):
        ab[step].wait_recv()
        own_sum = own_sum + asb_rx[step, :, 0:width].astype(F32)
        own_cnt = own_cnt + join_count(asb_rx[step, :, width:])
    first = (w * narrow + y) * shard
    cnt_row = counts[pl.ds(first // 128, 1), :]
    cnt_col[...] = jnp.transpose(jnp.broadcast_to(cnt_row, (128, 128)))
    if shard <= 128:
        old_cnt = cnt_col[pl.ds(pl.multiple_of(first % 128, shard), shard), :]
    else:
        old_cnt = jnp.concatenate(
            [jnp.transpose(jnp.broadcast_to(counts[pl.ds(first // 128 + b, 1), :], (128, 128))) for b in range(shard // 128)], 0
        )
    scale = 1.0 / (decay_rate * old_cnt + (1.0 - decay_rate) * own_cnt)
    old = sums[pl.ds(pl.multiple_of(first, shard), shard), :]
    for part in range(width // 128):
        lanes = slice(part * 128, part * 128 + 128)
        newcb[:, lanes] = (decay_rate * old[:, lanes] + (1.0 - decay_rate) * own_sum[:, lanes]) * scale

    ret[...] = dot_nt(dz_all[...], ws[...])
    acc[...] = dot(tab_code[:, 0:n], daggg[0:n, :])
    ret[...] += dot(tab_ret[:, 0:n], daggg[0:n, :]) * (1.0 / 8)
    arrived(daggg, d_s, d_r, 2)
    acc[...] += dot(tab_code[:, 3 * n : 4 * n], daggg[3 * n : 4 * n, :])
    ret[...] += dot(tab_ret[:, 3 * n : 4 * n], daggg[3 * n : 4 * n, :]) * (1.0 / 8)
    arrived(daggg, d_s, d_r, 3)
    acc[...] += dot(tab_code[:, n : 2 * n], daggg[n : 2 * n, :])
    ret[...] += dot(tab_ret[:, n : 2 * n], daggg[n : 2 * n, :]) * (1.0 / 8)
    arrived(daggg, d_s, d_r, 4)
    arrived(daggg, d_s, d_r, 5)
    last = daggg[2 * n : 3 * n, :]
    cg_tx[...] = ((acc[own_half:, :] + dot(tab_code[own_half:, 2 * n : 3 * n], last)) * (1.0 / 16)).astype(BF16)
    ca = rcopy(cg_tx, cg_rx, ca_s, ca_r, (other, y))
    ca.start()
    acc[0:own_half, :] = (acc[0:own_half, :] + dot(tab_code[0:own_half, 2 * n : 3 * n], last)) * (1.0 / 16)
    fgrad[...] = (ret[...] + dot(tab_ret[:, 2 * n : 3 * n], last) * (1.0 / 8)).astype(BF16)
    ca.wait_recv()
    cb = {}
    for step in range(1, chips):
        rows = pl.ds(step * shard, shard)
        cgb_tx[step] = (acc[rows, :] + cg_rx[rows, :].astype(F32)).astype(BF16)
        cb[step] = rcopy(cgb_tx.at[step], cgb_rx.at[step], cb_s.at[step], cb_r.at[step], (chip_dev(step), y))
        cb[step].start()

    def gathered(step, carry):
        source = (w + wide - step) % wide
        rcopy(
            wgd.at[share_rows(source), :], wgd.at[share_rows(source), :], wd_s.at[step], wd_r.at[step], (source, y)
        ).wait_recv()
        return carry

    lax.fori_loop(1, wide, gathered, 0)
    wrows = wg_own.shape[0]
    sgrad[...] = wgd[0:wrows, :].astype(F32)
    ngrad[...] = wgd[wrows:, :].astype(F32)

    own = acc[0:shard, :] + cg_rx[0:shard, :].astype(F32)
    for step in range(1, chips):
        cb[step].wait_recv()
        own = own + cgb_rx[step].astype(F32)
    cgrad[...] = own

    for copy in (*f_copies, *d_copies, *i_copies, wa, aa, ca, *wc):
        copy.wait_send()
    for step in range(1, chips):
        wb[step].wait_send()
        ab[step].wait_send()
        cb[step].wait_send()

    def sent(step, carry):
        rcopy(
            wgd.at[share_rows(w), :], wgd.at[share_rows(w), :], wd_s.at[step], wd_r.at[step], ((w + step) % wide, y)
        ).wait_send()
        return carry

    lax.fori_loop(1, wide, sent, 0)


def on_device(
    wide, narrow,
    features, neighbours, code_ids, assignment, cotangent, code_sums, code_counts, self_weight, neighbour_weight,
):
    n, width = features.shape
    codes = code_sums.shape[0]
    chips = wide // 2
    shard = codes // (wide * narrow)
    mine = codes // narrow
    grp = n * narrow
    vm = pl.BlockSpec(memory_space=pltpu.VMEM)
    dma = pltpu.SemaphoreType.DMA
    wide_rows = self_weight.shape[0]
    scratch = [
        pltpu.VMEM((codes, width), F32),
        pltpu.VMEM((codes, width), BF16),
        pltpu.VMEM((grp, width), BF16),
        pltpu.VMEM((grp, width), BF16),
        pltpu.VMEM((narrow, IDX_ROWS, n), I32),
        pltpu.VMEM((n, 128), I32),
        pltpu.VMEM((128, n), I32),
        pltpu.VMEM((n, codes), BF16),
        pltpu.VMEM((n, grp), BF16),
        pltpu.VMEM((mine, grp), BF16),
        pltpu.VMEM((n, grp), BF16),
        pltpu.VMEM((mine, grp), BF16),
        pltpu.VMEM((16, grp), I32),
        pltpu.VMEM((16, grp), I32),
        pltpu.VMEM((8, grp), I32),
        pltpu.VMEM((8, grp), I32),
        pltpu.VMEM((8, grp), I32),
        pltpu.VMEM((n, width), F32),
        pltpu.VMEM((n, width), F32),
        pltpu.VMEM((n, width), F32),
        pltpu.VMEM((n, width), BF16),
        pltpu.VMEM((n, width), BF16),
        pltpu.VMEM((mine, width), F32),
        pltpu.VMEM((n, width), F32),
        pltpu.VMEM((2, wide_rows, width), F32),
        pltpu.VMEM((wide_rows, width), BF16),
        pltpu.VMEM((wide_rows, width), BF16),
        pltpu.VMEM((wide_rows, width), BF16),
        pltpu.VMEM((chips, wide_rows // chips, width), BF16),
        pltpu.VMEM((narrow, wide_rows // chips, width), F32),
        pltpu.VMEM((2 * wide_rows, width), BF16),
        pltpu.VMEM((mine, width), F32),
        pltpu.VMEM((mine, 128), F32),
        pltpu.VMEM((mine // 2, width + 128), BF16),
        pltpu.VMEM((mine // 2, width + 128), BF16),
        pltpu.VMEM((chips, shard, width + 128), BF16),
        pltpu.VMEM((chips, shard, width + 128), BF16),
        pltpu.VMEM((mine // 2, width), BF16),
        pltpu.VMEM((mine // 2, width), BF16),
        pltpu.VMEM((chips, shard, width), BF16),
        pltpu.VMEM((chips, shard, width), BF16),
        pltpu.VMEM((128, 128), F32),
        dma,
        dma((6,)), dma((6,)), dma((6,)), dma((6,)), dma((3,)), dma((3,)),
        dma, dma, dma((chips,)), dma((chips,)), dma((3,)), dma((3,)), dma((wide,)), dma((wide,)),
        dma, dma, dma((chips,)), dma((chips,)), dma, dma, dma((chips,)), dma((chips,)),
    ]
    return pl.pallas_call(
        functools.partial(kernel, wide, narrow, shard),
        out_shape=(
            jax.ShapeDtypeStruct((n, width), BF16),
            jax.ShapeDtypeStruct((n, width), BF16),
            jax.ShapeDtypeStruct(self_weight.shape, F32),
            jax.ShapeDtypeStruct(neighbour_weight.shape, F32),
            jax.ShapeDtypeStruct((shard, width), F32),
            jax.ShapeDtypeStruct((shard, width), F32),
        ),
        in_specs=[vm] * 5 + [pl.BlockSpec(memory_space=pl.ANY)] + [vm] * 3,
        out_specs=(vm,) * 6,
        scratch_shapes=scratch,
        compiler_params=pltpu.CompilerParams(
            collective_id=0, has_side_effects=True, vmem_limit_bytes=58 * 1024 * 1024
        ),
    )(
        features, neighbours.T, code_ids.T, assignment.reshape(1, n), cotangent,
        code_sums, code_counts.reshape(codes // 128, 128), self_weight, neighbour_weight,
    )


def solution(mesh):
    both = ("wide", "narrow")
    return jax.shard_map(
        functools.partial(on_device, mesh.shape["wide"], mesh.shape["narrow"]),
        mesh=mesh,
        in_specs=(P(both, None), P(both, None), P(both, None), P(both), P(both, None), P(), P(), P(), P()),
        out_specs=(P(both, None), P(both, None), P(), P(), P(both, None), P(both, None)),
        check_vma=False,
    )
```

time: 324 us -> 72.7 us (0.22); the launches traced: 319 us -> 72.3 us
  waiting for transfers between devices: 119 us -> 0 us
  blocking collectives: 66.2 us -> 0 us
  Pallas kernels: 0 us -> 62.3 us
  matrix products: 50.7 us -> 0 us
  other arithmetic: 47.3 us -> 0 us
  between operations: 14.2 us -> 0.65 us
  local copies, waits for them, and re-layouts: 21.6 us -> 9.42 us
    psum x1 -> x0, waiting for transfers between devices: 104 us -> none  [on_device(): lax.psum((self_local, neighbour_local), ('wide', 'narrow'))]
    psum x1 -> x0, blocking collectives: 66.2 us -> none  [on_device(): lax.psum((assigned_sum, assigned_count, code_local), ('wide', 'narrow'))]
    pallas_call x0 -> x1, Pallas kernels: none -> 62.3 us  [on_device(): pl.pallas_call(functools.partial(kernel, wide, narrow, shard), out_shape=...]
    dot_general x9 -> x0, matrix products: 50.7 us -> none  [the longest x1 19.7 us: grad_block(): jnp.einsum('bk,bf->kf', pick_table(block_ids), block_grad, preferred_elem...]
    scatter-add x8 -> x0, other arithmetic: 33.9 us -> none  [on_device(): term.at[jnp.clip(relative, 0, node_rows * lax.axis_size('narrow') - 1)]]
    gather x1 -> x0, local copies, waits for them, and re-layouts: 14.3 us -> none  [on_device(): taken_rows = jnp.take(piece_rows, jnp.clip(relative, 0, length - 1), axis=0)]
    all_gather x1 -> x0, waiting for transfers between devices: 14.2 us -> none  [on_device(): piece_rows = lax.all_gather(features, 'narrow', axis=0, tiled=True)]
    reduce_sum x2 -> x0, other arithmetic: 5.4 us -> none  [the longest x1 3.41 us: on_device(): near = jnp.sum(kept_rows, axis=1)]
  transfers between devices with their start and end apart: 3 -> 0, of which waited for: 2 -> 0; matrix products, arithmetic and copies ran while one was open for 12% -> 0% of each run, Pallas kernels for 0% -> 0%
where the time goes in v1:
time: 72.7 us; the launch traced here: 72.3 us
  Pallas kernels  62.3 us (86%)
  local copies, waits for them, and re-layouts  9.42 us (13%)
    pallas_call x1, Pallas kernels, on_device(): pl.pallas_call(functools.partial(kernel, wide, narrow, shard), out_shape=...  62.3 us
    unnamed x6, local copies, waits for them, and re-layouts  9.42 us

profile of v1, /device:TPU:1, one launch (start us, length us, event | category | flops | bytes accessed | tf_op | source)
XLA Modules:
  0.0 72.3 jit_solution(14237076700063251362)
XLA Ops:
  0.6 62.3 %shard_map.136 = (bf16[512,256]{1,0:T(8,128)(2,1)}, bf16[512,256]{1,0:T(8,128)(2,1)}, f32[256,256]{1,0:T(8,128)}, f32[256,256]{1,0:T(8,128)}, f32[32,256]{1,0:T(8,128)}, /*index=5*/f32[32,256]{1,0:T(8,128)}) custom-call(bf16[512,256]{1,0:T(8,128)(2,1)} %feat.1, s32[8,512]{1,0:T(8,128)} %bitcast.5, s32[16,512]{1,0:T(8,128)} %bitcast.4, s32[1,512]{1,0:T(1,128)} %bitcast.7, ...), custom_call_target="tpu_custom_call" | custom-call | tf_op jit(solution)/shard_map/pallas_call | solution.py:517
  62.9 1.7 %copy.21 = bf16[512,256]{1,0:T(8,128)(2,1)} copy(bf16[512,256]{1,0:T(8,128)(2,1)} %get-tuple-element.12) | data formatting | bytes 524288
  64.6 1.7 %copy.22 = bf16[512,256]{1,0:T(8,128)(2,1)} copy(bf16[512,256]{1,0:T(8,128)(2,1)} %get-tuple-element.13) | data formatting | bytes 524288
  66.2 1.7 %copy.23 = f32[256,256]{1,0:T(8,128)} copy(f32[256,256]{1,0:T(8,128)} %get-tuple-element.14) | data formatting | bytes 524288
  67.9 1.7 %copy.24 = f32[256,256]{1,0:T(8,128)} copy(f32[256,256]{1,0:T(8,128)} %get-tuple-element.15) | data formatting | bytes 524288
  69.6 1.4 %copy.25 = f32[32,256]{1,0:T(8,128)} copy(f32[32,256]{1,0:T(8,128)} %get-tuple-element.16) | data formatting | bytes 65536
  71.0 1.4 %copy.26 = f32[32,256]{1,0:T(8,128)} copy(f32[32,256]{1,0:T(8,128)} %get-tuple-element.17) | data formatting | bytes 65536

commit v2 on v1

--- a/solution.py
+++ b/solution.py
@@ -54,16 +54,17 @@
 
 def kernel(
     wide, narrow, shard,
-    feat, nb_t, code_t, assign, cot, sums_hbm, counts, ws, wn,
-    out, fgrad, sgrad, ngrad, newcb, cgrad,
-    sums, codebook, featg, daggg, idxg, ids_nt, idx_pad, tab_far, tab_near, tab_code, tab_ret, tab_asn,
-    hi_t, val_t, hi_r, val_r, row_a, far, near, hid, dz_all, agg_all, acc, ret,
-    wg_f, wg_tx, wg_rx, wgb_tx, wgb_rx, wgc, wgd, as_f, as_cnt, as_tx, as_rx, asb_tx, asb_rx,
+    feat_hbm, nb_hbm, code_hbm, assign_hbm, cot_hbm, sums_hbm, counts_hbm, ws_hbm, wn_hbm,
+    out_hbm, fgrad_hbm, sgrad_hbm, ngrad_hbm, newcb_hbm, cgrad_hbm,
+    cot, sums, counts, ws, wn, out, fgrad, wgrads, newcb, cgrad,
+    codebook, featg, daggg, idxg, tab_far, tab_near, tab_code, tab_ret, tab_asn,
+    hi_f, val_f, hi_n, val_n, hi_t, val_t, hi_r, val_r, row_a, far, near, hid, dz_all, agg_all, acc, ret,
+    wg_f, wg_tx, wg_rx, wgb_tx, wgb_rx, wgc, wgd, as_f, as_cnt, as_acc, as_tx, as_rx, asb_tx, asb_rx,
     cg_tx, cg_rx, cgb_tx, cgb_rx, cnt_col,
-    sums_sem, f_s, f_r, d_s, d_r, i_s, i_r, wa_s, wa_r, wb_s, wb_r, wc_s, wc_r, wd_s, wd_r,
+    in_sem, out_sem, f_s, f_r, d_s, d_r, i_s, i_r, wa_s, wa_r, wb_s, wb_r, wc_s, wc_r, wd_s, wd_r,
     aa_s, aa_r, ab_s, ab_r, ca_s, ca_r, cb_s, cb_r,
 ):
-    n = feat.shape[0]
+    n = cot.shape[0]
     half = n // 2
     chips = wide // 2
     codes = sums.shape[0]
@@ -85,8 +86,26 @@
             src_ref=src, dst_ref=dst, send_sem=ssem, recv_sem=rsem, device_id=dev, device_id_type=MESH
         )
 
-    sums_copy = pltpu.make_async_copy(sums_hbm, sums, sums_sem)
-    sums_copy.start()
+    feat = featg.at[pl.ds(0, n), :]
+    idxg[0, 24:32, :] = jnp.zeros((8, n), I32)
+    fetched = [
+        pltpu.make_async_copy(src, dst, in_sem.at[at])
+        for at, (src, dst) in enumerate(
+            (
+                (feat_hbm, feat),
+                (nb_hbm, idxg.at[0, pl.ds(0, 8), :]),
+                (code_hbm, idxg.at[0, pl.ds(8, 16), :]),
+                (assign_hbm, idxg.at[0, pl.ds(24, 1), :]),
+                (counts_hbm, counts),
+                (sums_hbm, sums),
+                (ws_hbm, ws),
+                (wn_hbm, wn),
+                (cot_hbm, cot),
+            )
+        )
+    ]
+    for copy in fetched:
+        copy.start()
 
     barrier = pltpu.get_barrier_semaphore()
     for peer in (y_right, y_left, y_far):
@@ -97,19 +116,8 @@
         return carry
 
     lax.fori_loop(1, wide, greet, 0)
-
-    featg[pl.ds(0, n), :] = feat[...]
-    idxg[0, 0:8, :] = nb_t[...]
-    idxg[0, 8:24, :] = code_t[...]
-    idxg[0, 24:32, :] = jnp.broadcast_to(assign[...], (8, n))
-    idx_pad[...] = jnp.zeros_like(idx_pad)
-    nb_own = nb_t[...]
-    node_bits = n.bit_length() - 1
-    slot_of = ((nb_own >> node_bits) - y) & (narrow - 1)
-    idx_pad[0:8, :] = (slot_of << node_bits) | (nb_own & (n - 1))
-    idx_pad[8:24, :] = code_t[...]
-    ids_nt[...] = jnp.transpose(idx_pad[...])
-
+    for at in range(4):
+        fetched[at].wait()
     pl.semaphore_wait(barrier, narrow - 1 + wide - 1)
 
     def low(slot):
@@ -145,71 +153,72 @@
         i_copies.append(rcopy(idxg.at[0], idxg.at[slot], i_s.at[at], i_r.at[at], (w, peer)))
         i_copies[-1].start()
 
+    def table(tab, his_ref, vals_ref, spots_in, lane_at, first_spot):
+        lanes = pl.ds(pl.multiple_of(lane_at, 128), 128)
+        picks = his_ref.shape[0]
+        his = [jnp.broadcast_to(his_ref[j : j + 1, lanes], (16, 128)) for j in range(picks)]
+        vals = [jnp.broadcast_to(vals_ref[j : j + 1, lanes], (16, 128)) for j in range(picks)]
+        base = lax.broadcasted_iota(I32, (16, 128), 0) + first_spot
+        for part in range(min(spots_in, 128) // 16):
+            spots = base + part * 16
+            words = [words_of(spots, his[at : at + 8], vals[at : at + 8]) for at in range(0, picks, 8)]
+            for field, counts_part in enumerate(fields_of(words)):
+                row = pl.multiple_of(field * spots_in + part * 16 + first_spot, 16)
+                tab[pl.ds(row, 16), lanes] = counts_part
+
     far_spots = codes // 8
     far_bits = far_spots.bit_length() - 1
     near_spots = grp // 8
     near_bits = near_spots.bit_length() - 1
+    node_bits = n.bit_length() - 1
+    own_ids = idxg[0, 8:24, :]
+    hi_f[...] = own_ids & (far_spots - 1)
+    val_f[...] = jnp.int32(1) << ((own_ids >> far_bits) * 4)
+    own_ids = idxg[0, 0:8, :]
+    own_ids = ((((own_ids >> node_bits) - y) & (narrow - 1)) << node_bits) | (own_ids & (n - 1))
+    hi_n[...] = own_ids & (near_spots - 1)
+    val_n[...] = jnp.int32(1) << ((own_ids >> near_bits) * 4)
 
     def far_tile(tile, carry):
-        rows = pl.ds(pl.multiple_of(tile * 16, 16), 16)
-        ids = ids_nt[rows, :]
-        hi = ids & (far_spots - 1)
-        val = jnp.int32(1) << ((ids >> far_bits) * 4)
-        his = [jnp.broadcast_to(hi[:, 8 + j : 9 + j], (16, 128)) for j in range(16)]
-        vals = [jnp.broadcast_to(val[:, 8 + j : 9 + j], (16, 128)) for j in range(16)]
-        for part in range(far_spots // 128):
-            spots = lax.broadcasted_iota(I32, (16, 128), 1) + part * 128
-            words = (words_of(spots, his[:8], vals[:8]), words_of(spots, his[8:], vals[8:]))
-            for field, counts_part in enumerate(fields_of(words)):
-                tab_far[rows, pl.ds(field * far_spots + part * 128, 128)] = counts_part
+        table(tab_far, hi_f, val_f, far_spots, (tile // (far_spots // 128)) * 128, (tile % (far_spots // 128)) * 128)
         return carry
 
     def near_tile(tile, carry):
-        rows = pl.ds(pl.multiple_of(tile * 16, 16), 16)
-        ids = ids_nt[rows, :]
-        hi = ids & (near_spots - 1)
-        val = jnp.int32(1) << ((ids >> near_bits) * 4)
-        his = [jnp.broadcast_to(hi[:, j : j + 1], (16, 128)) for j in range(8)]
-        vals = [jnp.broadcast_to(val[:, j : j + 1], (16, 128)) for j in range(8)]
-        for part in range(near_spots // 128):
-            spots = lax.broadcasted_iota(I32, (16, 128), 1) + part * 128
-            words = (words_of(spots, his, vals),)
-            for field, counts_part in enumerate(fields_of(words)):
-                tab_near[rows, pl.ds(field * near_spots + part * 128, 128)] = counts_part
-        return carry
-
-    def book_block(block, carry):
-        rows = pl.ds(pl.multiple_of(block * 128, 128), 128)
-        inverse = 1.0 / counts[pl.ds(block, 1), :]
-        column = jnp.transpose(jnp.broadcast_to(inverse, (128, 128)))
-        for part in range(sums.shape[1] // 128):
-            lanes = pl.ds(part * 128, 128)
-            codebook[rows, lanes] = (sums[rows, lanes] * column).astype(BF16)
-        return carry
-
-    lax.fori_loop(0, n // 32, far_tile, 0)
+        table(tab_near, hi_n, val_n, near_spots, (tile // (near_spots // 128)) * 128, (tile % (near_spots // 128)) * 128)
+        return carry
+
+    far_tiles = (n // 128) * (far_spots // 128)
+    lax.fori_loop(0, far_tiles // 2, far_tile, 0)
     arrived(featg, f_s, f_r, 0)
     f_copies[4].start()
     arrived(featg, f_s, f_r, 1)
     f_copies[5].start()
-    lax.fori_loop(n // 32, n // 16, far_tile, 0)
-    sums_copy.wait()
-    lax.fori_loop(0, codes // 128, book_block, 0)
-    far[...] = dot(tab_far[...], codebook[...]) * (1.0 / 16)
-    lax.fori_loop(0, n // 16, near_tile, 0)
+    lax.fori_loop(far_tiles // 2, far_tiles, far_tile, 0)
+    width = sums.shape[1]
+    for at in range(4, 9):
+        fetched[at].wait()
+    blocks = codes // 128
+    inverse = jnp.transpose(jnp.concatenate([1.0 / counts[...]] * (128 // blocks), 0))
+    for block in range(blocks):
+        column = jnp.broadcast_to(inverse[:, block : block + 1], (128, 128))
+        for part in range(width // 128):
+            at = (slice(block * 128, block * 128 + 128), slice(part * 128, part * 128 + 128))
+            codebook[at] = (sums[at] * column).astype(BF16)
+    far[...] = dot_tn(tab_far[...], codebook[...]) * (1.0 / 16)
+    lax.fori_loop(0, (n // 128) * (near_spots // 128), near_tile, 0)
     hid[...] = dot(feat[...], ws[...])
-    near[...] = dot(tab_near[:, 0:n], feat[...])
+    near[...] = dot_tn(tab_near[0:n, :], feat[...])
     arrived(featg, f_s, f_r, 2)
-    near[...] += dot(tab_near[:, 3 * n : 4 * n], featg[3 * n : 4 * n, :])
+    near[...] += dot_tn(tab_near[3 * n : 4 * n, :], featg[3 * n : 4 * n, :])
     arrived(featg, f_s, f_r, 3)
-    near[...] += dot(tab_near[:, n : 2 * n], featg[n : 2 * n, :])
+    near[...] += dot_tn(tab_near[n : 2 * n, :], featg[n : 2 * n, :])
     arrived(featg, f_s, f_r, 4)
     arrived(featg, f_s, f_r, 5)
 
     d_copies = gather_copies(daggg, d_s, d_r)
     for at in range(2):
         rows = pl.ds(at * half, half)
-        total = near[rows, :] + dot(tab_near[rows, 2 * n : 3 * n], featg[2 * n : 3 * n, :])
+        total = near[rows, :] + dot_tn(tab_near[2 * n : 3 * n, at * half : at * half + half], featg[2 * n : 3 * n, :])
         agg = (total * (1.0 / 8) + far[rows, :]).astype(BF16)
         agg_all[rows, :] = agg
         z = hid[rows, :] + dot(agg, wn[...])
@@ -220,6 +229,16 @@
         daggg[rows, :] = dot_nt(dz, wn[...]).astype(BF16)
         d_copies[(0, 1)[at]].start()
         d_copies[(3, 2)[at]].start()
+    written = [
+        pltpu.make_async_copy(src, dst, out_sem.at[at])
+        for at, (src, dst) in enumerate(
+            (
+                (out, out_hbm), (fgrad, fgrad_hbm), (wgrads.at[0], sgrad_hbm),
+                (wgrads.at[1], ngrad_hbm), (newcb, newcb_hbm), (cgrad, cgrad_hbm),
+            )
+        )
+    ]
+    written[0].start()
 
     def weight_half(which, x):
         wg_f[which] = dot_tn(x, dz_all[...])
@@ -256,34 +275,24 @@
         row, hit = place(idxg[slot, 24:32, :])
         row_a[:, lanes] = jnp.where(hit, row, -1)
 
-    def asn_tile(tile, carry):
-        lanes = pl.ds(pl.multiple_of(tile * 128, 128), 128)
-        row = jnp.broadcast_to(row_a[0:1, lanes], (16, 128))
-        for part in range(mine // 16):
-            spots = lax.broadcasted_iota(I32, (16, 128), 0) + part * 16
-            tab_asn[pl.ds(part * 16, 16), lanes] = jnp.where(row == spots, 1.0, 0.0).astype(BF16)
+    def asn_part(part, carry):
+        rows = pl.ds(pl.multiple_of(part * 16, 16), 16)
+        spots = lax.broadcasted_iota(I32, (16, 128), 0) + part * 16
+        total = None
+        for tile in range(grp // 128):
+            lanes = slice(tile * 128, tile * 128 + 128)
+            hit = jnp.where(jnp.broadcast_to(row_a[0:1, lanes], (16, 128)) == spots, 1.0, 0.0)
+            tab_asn[rows, lanes] = hit.astype(BF16)
+            total = hit if total is None else total + hit
+        as_acc[rows, :] = total.astype(BF16)
         return carry
 
     def code_tile(tile, carry):
-        lanes = pl.ds(pl.multiple_of(tile * 128, 128), 128)
-        his = [jnp.broadcast_to(hi_t[j : j + 1, lanes], (16, 128)) for j in range(16)]
-        vals = [jnp.broadcast_to(val_t[j : j + 1, lanes], (16, 128)) for j in range(16)]
-        for part in range(mine_spots // 16):
-            spots = lax.broadcasted_iota(I32, (16, 128), 0) + part * 16
-            words = (words_of(spots, his[:8], vals[:8]), words_of(spots, his[8:], vals[8:]))
-            for field, counts_part in enumerate(fields_of(words)):
-                tab_code[pl.ds(field * mine_spots + part * 16, 16), lanes] = counts_part
+        table(tab_code, hi_t, val_t, mine_spots, tile * 128, 0)
         return carry
 
     def ret_tile(tile, carry):
-        lanes = pl.ds(pl.multiple_of(tile * 128, 128), 128)
-        his = [jnp.broadcast_to(hi_r[j : j + 1, lanes], (16, 128)) for j in range(8)]
-        vals = [jnp.broadcast_to(val_r[j : j + 1, lanes], (16, 128)) for j in range(8)]
-        for part in range(ret_spots // 16):
-            spots = lax.broadcasted_iota(I32, (16, 128), 0) + part * 16
-            words = (words_of(spots, his, vals),)
-            for field, counts_part in enumerate(fields_of(words)):
-                tab_ret[pl.ds(field * ret_spots + part * 16, 16), lanes] = counts_part
+        table(tab_ret, hi_r, val_r, ret_spots, tile * 128, 0)
         return carry
 
     def split_count(count):
@@ -295,10 +304,9 @@
         pair = pair.astype(F32)
         return pair + pltpu.roll(pair, 64, 1)
 
-    width = feat.shape[1]
-    lax.fori_loop(0, grp // 128, asn_tile, 0)
+    lax.fori_loop(0, mine // 16, asn_part, 0)
     as_f[...] = dot(tab_asn[...], featg[...])
-    as_cnt[...] = dot(tab_asn[...], jnp.ones((grp, 128), BF16))
+    as_cnt[...] = dot(as_acc[...], jnp.ones((128, 128), BF16))
     as_tx[:, 0:width] = as_f[own_half:, :].astype(BF16)
     as_tx[:, width:] = split_count(as_cnt[own_half:, :])
     aa = rcopy(as_tx, as_rx, aa_s, aa_r, (other, y))
@@ -393,6 +401,7 @@
     for part in range(width // 128):
         lanes = slice(part * 128, part * 128 + 128)
         newcb[:, lanes] = (decay_rate * old[:, lanes] + (1.0 - decay_rate) * own_sum[:, lanes]) * scale
+    written[4].start()
 
     ret[...] = dot_nt(dz_all[...], ws[...])
     acc[...] = dot(tab_code[:, 0:n], daggg[0:n, :])
@@ -411,6 +420,7 @@
     ca.start()
     acc[0:own_half, :] = (acc[0:own_half, :] + dot(tab_code[0:own_half, 2 * n : 3 * n], last)) * (1.0 / 16)
     fgrad[...] = (ret[...] + dot(tab_ret[:, 2 * n : 3 * n], last) * (1.0 / 8)).astype(BF16)
+    written[1].start()
     ca.wait_recv()
     cb = {}
     for step in range(1, chips):
@@ -428,14 +438,17 @@
 
     lax.fori_loop(1, wide, gathered, 0)
     wrows = wg_own.shape[0]
-    sgrad[...] = wgd[0:wrows, :].astype(F32)
-    ngrad[...] = wgd[wrows:, :].astype(F32)
+    wgrads[0] = wgd[0:wrows, :].astype(F32)
+    wgrads[1] = wgd[wrows:, :].astype(F32)
+    written[2].start()
+    written[3].start()
 
     own = acc[0:shard, :] + cg_rx[0:shard, :].astype(F32)
     for step in range(1, chips):
         cb[step].wait_recv()
         own = own + cgb_rx[step].astype(F32)
     cgrad[...] = own
+    written[5].start()
 
     for copy in (*f_copies, *d_copies, *i_copies, wa, aa, ca, *wc):
         copy.wait_send()
@@ -451,6 +464,17 @@
         return carry
 
     lax.fori_loop(1, wide, sent, 0)
+    for copy in written:
+        copy.wait()
+
+
+def copy_kernel(*refs):
+    count = len(refs) // 2
+    copies = [pltpu.make_async_copy(refs[at], refs[count + at], refs[-1].at[at]) for at in range(count)]
+    for copy in copies:
+        copy.start()
+    for copy in copies:
+        copy.wait()
 
 
 def on_device(
@@ -463,22 +487,33 @@
     shard = codes // (wide * narrow)
     mine = codes // narrow
     grp = n * narrow
-    vm = pl.BlockSpec(memory_space=pltpu.VMEM)
+    hbm = pl.BlockSpec(memory_space=pl.ANY)
     dma = pltpu.SemaphoreType.DMA
     wide_rows = self_weight.shape[0]
     scratch = [
+        pltpu.VMEM((n, width), BF16),
         pltpu.VMEM((codes, width), F32),
+        pltpu.VMEM((codes // 128, 128), F32),
+        pltpu.VMEM(self_weight.shape, BF16),
+        pltpu.VMEM(neighbour_weight.shape, BF16),
+        pltpu.VMEM((n, width), BF16),
+        pltpu.VMEM((n, width), BF16),
+        pltpu.VMEM((2, *self_weight.shape), F32),
+        pltpu.VMEM((shard, width), F32),
+        pltpu.VMEM((shard, width), F32),
         pltpu.VMEM((codes, width), BF16),
         pltpu.VMEM((grp, width), BF16),
         pltpu.VMEM((grp, width), BF16),
         pltpu.VMEM((narrow, IDX_ROWS, n), I32),
-        pltpu.VMEM((n, 128), I32),
-        pltpu.VMEM((128, n), I32),
-        pltpu.VMEM((n, codes), BF16),
-        pltpu.VMEM((n, grp), BF16),
+        pltpu.VMEM((codes, n), BF16),
+        pltpu.VMEM((grp, n), BF16),
         pltpu.VMEM((mine, grp), BF16),
         pltpu.VMEM((n, grp), BF16),
         pltpu.VMEM((mine, grp), BF16),
+        pltpu.VMEM((16, n), I32),
+        pltpu.VMEM((16, n), I32),
+        pltpu.VMEM((8, n), I32),
+        pltpu.VMEM((8, n), I32),
         pltpu.VMEM((16, grp), I32),
         pltpu.VMEM((16, grp), I32),
         pltpu.VMEM((8, grp), I32),
@@ -500,6 +535,7 @@
         pltpu.VMEM((2 * wide_rows, width), BF16),
         pltpu.VMEM((mine, width), F32),
         pltpu.VMEM((mine, 128), F32),
+        pltpu.VMEM((mine, 128), BF16),
         pltpu.VMEM((mine // 2, width + 128), BF16),
         pltpu.VMEM((mine // 2, width + 128), BF16),
         pltpu.VMEM((chips, shard, width + 128), BF16),
@@ -509,23 +545,24 @@
         pltpu.VMEM((chips, shard, width), BF16),
         pltpu.VMEM((chips, shard, width), BF16),
         pltpu.VMEM((128, 128), F32),
-        dma,
+        dma((9,)), dma((6,)),
         dma((6,)), dma((6,)), dma((6,)), dma((6,)), dma((3,)), dma((3,)),
         dma, dma, dma((chips,)), dma((chips,)), dma((3,)), dma((3,)), dma((wide,)), dma((wide,)),
         dma, dma, dma((chips,)), dma((chips,)), dma, dma, dma((chips,)), dma((chips,)),
     ]
-    return pl.pallas_call(
+    shapes = (
+        jax.ShapeDtypeStruct((n, width), BF16),
+        jax.ShapeDtypeStruct((n, width), BF16),
+        jax.ShapeDtypeStruct(self_weight.shape, F32),
+        jax.ShapeDtypeStruct(neighbour_weight.shape, F32),
+        jax.ShapeDtypeStruct((shard, width), F32),
+        jax.ShapeDtypeStruct((shard, width), F32),
+    )
+    results = pl.pallas_call(
         functools.partial(kernel, wide, narrow, shard),
-        out_shape=(
-            jax.ShapeDtypeStruct((n, width), BF16),
-            jax.ShapeDtypeStruct((n, width), BF16),
-            jax.ShapeDtypeStruct(self_weight.shape, F32),
-            jax.ShapeDtypeStruct(neighbour_weight.shape, F32),
-            jax.ShapeDtypeStruct((shard, width), F32),
-            jax.ShapeDtypeStruct((shard, width), F32),
-        ),
-        in_specs=[vm] * 5 + [pl.BlockSpec(memory_space=pl.ANY)] + [vm] * 3,
-        out_specs=(vm,) * 6,
+        out_shape=shapes,
+        in_specs=[hbm] * 9,
+        out_specs=(hbm,) * 6,
         scratch_shapes=scratch,
         compiler_params=pltpu.CompilerParams(
             collective_id=0, has_side_effects=True, vmem_limit_bytes=58 * 1024 * 1024
@@ -534,6 +571,14 @@
         features, neighbours.T, code_ids.T, assignment.reshape(1, n), cotangent,
         code_sums, code_counts.reshape(codes // 128, 128), self_weight, neighbour_weight,
     )
+    return pl.pallas_call(
+        copy_kernel,
+        out_shape=shapes,
+        in_specs=[hbm] * 6,
+        out_specs=(hbm,) * 6,
+        scratch_shapes=[dma((6,))],
+        compiler_params=pltpu.CompilerParams(vmem_limit_bytes=62 * 1024 * 1024),
+    )(*results)
 
 
 def solution(mesh):

time: 72.7 us -> 90.7 us (1.25)
  Pallas kernels: 62.3 us -> 90 us
  local copies, waits for them, and re-layouts: 9.42 us -> 0 us
    pallas_call x0 -> x1, Pallas kernels: none -> 34.9 us  [on_device(): pl.pallas_call(copy_kernel, out_shape=shapes, in_specs=[hbm] * 6, out_spe...]
    unnamed x6 -> x0, local copies, waits for them, and re-layouts: 9.42 us -> none
    pallas_call x1, Pallas kernels: 62.3 us -> 55 us  [on_device(): pl.pallas_call(functools.partial(kernel, wide, narrow, shard), out_shape=...]
where the time goes in v2:
time: 90.7 us; the launch traced here: 90.6 us
  Pallas kernels  90 us (99%)
    pallas_call x1, Pallas kernels, on_device(): pl.pallas_call(functools.partial(kernel, wide, narrow, shard), out_shape=...  55 us
    pallas_call x1, Pallas kernels, on_device(): pl.pallas_call(copy_kernel, out_shape=shapes, in_specs=[hbm] * 6, out_spe...  34.9 us

profile of v2, /device:TPU:1, one launch (start us, length us, event | category | flops | bytes accessed | tf_op | source)
XLA Modules:
  0.0 90.6 jit_solution(707466360021896043)
XLA Ops:
  0.6 55.0 %shard_map.136 = (bf16[512,256]{1,0:T(8,128)(2,1)}, bf16[512,256]{1,0:T(8,128)(2,1)}, f32[256,256]{1,0:T(8,128)}, f32[256,256]{1,0:T(8,128)}, f32[32,256]{1,0:T(8,128)}, /*index=5*/f32[32,256]{1,0:T(8,128)}) custom-call(bf16[512,256]{1,0:T(8,128)(2,1)} %feat_hbm.1, s32[8,512]{1,0:T(8,128)} %bitcast.5, s32[16,512]{1,0:T(8,128)} %bitcast.4, s32[1,512]{1,0:T(1,128)} %bitcast.7, ...), custom_call_target="tpu_custom_call" | custom-call | tf_op jit(solution)/shard_map/pallas_call | solution.py:561
  55.7 34.9 %shard_map.137 = (bf16[512,256]{1,0:T(8,128)(2,1)}, bf16[512,256]{1,0:T(8,128)(2,1)}, f32[256,256]{1,0:T(8,128)}, f32[256,256]{1,0:T(8,128)}, f32[32,256]{1,0:T(8,128)}, /*index=5*/f32[32,256]{1,0:T(8,128)}) custom-call(bf16[512,256]{1,0:T(8,128)(2,1)} %get-tuple-element.12.refs_0_, bf16[512,256]{1,0:T(8,128)(2,1)} %get-tuple-element.13.refs_1_, ...), custom_call_target="tpu_custom_call" | custom-call | tf_op jit(solution)/shard_map/pallas_call | solution.py:574

commit v3 on v2

--- a/solution.py
+++ b/solution.py
@@ -55,13 +55,13 @@
 def kernel(
     wide, narrow, shard,
     feat_hbm, nb_hbm, code_hbm, assign_hbm, cot_hbm, sums_hbm, counts_hbm, ws_hbm, wn_hbm,
-    out_hbm, fgrad_hbm, sgrad_hbm, ngrad_hbm, newcb_hbm, cgrad_hbm,
-    cot, sums, counts, ws, wn, out, fgrad, wgrads, newcb, cgrad,
-    codebook, featg, daggg, idxg, tab_far, tab_near, tab_code, tab_ret, tab_asn,
+    out, fgrad, sgrad, ngrad, newcb, cgrad,
+    cot, sums, counts, ws, wn,
+    codebook, featg, daggg, idx_own, idxg, tab_far, tab_near, tab_code, tab_ret, tab_asn,
     hi_f, val_f, hi_n, val_n, hi_t, val_t, hi_r, val_r, row_a, far, near, hid, dz_all, agg_all, acc, ret,
     wg_f, wg_tx, wg_rx, wgb_tx, wgb_rx, wgc, wgd, as_f, as_cnt, as_acc, as_tx, as_rx, asb_tx, asb_rx,
     cg_tx, cg_rx, cgb_tx, cgb_rx, cnt_col,
-    in_sem, out_sem, f_s, f_r, d_s, d_r, i_s, i_r, wa_s, wa_r, wb_s, wb_r, wc_s, wc_r, wd_s, wd_r,
+    in_sem, f_s, f_r, d_s, d_r, i_s, i_r, wa_s, wa_r, wb_s, wb_r, wc_s, wc_r, wd_s, wd_r,
     aa_s, aa_r, ab_s, ab_r, ca_s, ca_r, cb_s, cb_r,
 ):
     n = cot.shape[0]
@@ -87,15 +87,15 @@
         )
 
     feat = featg.at[pl.ds(0, n), :]
-    idxg[0, 24:32, :] = jnp.zeros((8, n), I32)
+    idx_own[24:32, :] = jnp.zeros((8, n), I32)
     fetched = [
         pltpu.make_async_copy(src, dst, in_sem.at[at])
         for at, (src, dst) in enumerate(
             (
                 (feat_hbm, feat),
-                (nb_hbm, idxg.at[0, pl.ds(0, 8), :]),
-                (code_hbm, idxg.at[0, pl.ds(8, 16), :]),
-                (assign_hbm, idxg.at[0, pl.ds(24, 1), :]),
+                (nb_hbm, idx_own.at[pl.ds(0, 8), :]),
+                (code_hbm, idx_own.at[pl.ds(8, 16), :]),
+                (assign_hbm, idx_own.at[pl.ds(24, 1), :]),
                 (counts_hbm, counts),
                 (sums_hbm, sums),
                 (ws_hbm, ws),
@@ -148,10 +148,11 @@
     f_copies = gather_copies(featg, f_s, f_r)
     for at in range(4):
         f_copies[at].start()
-    i_copies = []
-    for at, (peer, slot) in enumerate(((y_right, 3), (y_left, 1), (y_far, 2))):
-        i_copies.append(rcopy(idxg.at[0], idxg.at[slot], i_s.at[at], i_r.at[at], (w, peer)))
-        i_copies[-1].start()
+    idxg[0] = idx_own[...].astype(jnp.int16)
+    i_copies = [
+        rcopy(idxg.at[0], idxg.at[slot], i_s.at[at], i_r.at[at], (w, peer))
+        for at, (peer, slot) in enumerate(((y_right, 3), (y_left, 1), (y_far, 2)))
+    ]
 
     def table(tab, his_ref, vals_ref, spots_in, lane_at, first_spot):
         lanes = pl.ds(pl.multiple_of(lane_at, 128), 128)
@@ -171,10 +172,10 @@
     near_spots = grp // 8
     near_bits = near_spots.bit_length() - 1
     node_bits = n.bit_length() - 1
-    own_ids = idxg[0, 8:24, :]
+    own_ids = idx_own[8:24, :]
     hi_f[...] = own_ids & (far_spots - 1)
     val_f[...] = jnp.int32(1) << ((own_ids >> far_bits) * 4)
-    own_ids = idxg[0, 0:8, :]
+    own_ids = idx_own[0:8, :]
     own_ids = ((((own_ids >> node_bits) - y) & (narrow - 1)) << node_bits) | (own_ids & (n - 1))
     hi_n[...] = own_ids & (near_spots - 1)
     val_n[...] = jnp.int32(1) << ((own_ids >> near_bits) * 4)
@@ -193,6 +194,8 @@
     f_copies[4].start()
     arrived(featg, f_s, f_r, 1)
     f_copies[5].start()
+    for copy in i_copies:
+        copy.start()
     lax.fori_loop(far_tiles // 2, far_tiles, far_tile, 0)
     width = sums.shape[1]
     for at in range(4, 9):
@@ -204,8 +207,17 @@
         for part in range(width // 128):
             at = (slice(block * 128, block * 128 + 128), slice(part * 128, part * 128 + 128))
             codebook[at] = (sums[at] * column).astype(BF16)
-    far[...] = dot_tn(tab_far[...], codebook[...]) * (1.0 / 16)
-    lax.fori_loop(0, (n // 128) * (near_spots // 128), near_tile, 0)
+    far[...] = jnp.zeros_like(far)
+    near_tiles = (n // 128) * (near_spots // 128)
+    step_codes = codes // near_tiles
+
+    def near_step(tile, carry):
+        near_tile(tile, 0)
+        rows = pl.ds(pl.multiple_of(tile * step_codes, step_codes), step_codes)
+        far[...] += dot_tn(tab_far[rows, :], codebook[rows, :])
+        return carry
+
+    lax.fori_loop(0, near_tiles, near_step, 0)
     hid[...] = dot(feat[...], ws[...])
     near[...] = dot_tn(tab_near[0:n, :], feat[...])
     arrived(featg, f_s, f_r, 2)
@@ -219,7 +231,7 @@
     for at in range(2):
         rows = pl.ds(at * half, half)
         total = near[rows, :] + dot_tn(tab_near[2 * n : 3 * n, at * half : at * half + half], featg[2 * n : 3 * n, :])
-        agg = (total * (1.0 / 8) + far[rows, :]).astype(BF16)
+        agg = (total * (1.0 / 8) + far[rows, :] * (1.0 / 16)).astype(BF16)
         agg_all[rows, :] = agg
         z = hid[rows, :] + dot(agg, wn[...])
         s = jax.nn.sigmoid(z)
@@ -229,16 +241,6 @@
         daggg[rows, :] = dot_nt(dz, wn[...]).astype(BF16)
         d_copies[(0, 1)[at]].start()
         d_copies[(3, 2)[at]].start()
-    written = [
-        pltpu.make_async_copy(src, dst, out_sem.at[at])
-        for at, (src, dst) in enumerate(
-            (
-                (out, out_hbm), (fgrad, fgrad_hbm), (wgrads.at[0], sgrad_hbm),
-                (wgrads.at[1], ngrad_hbm), (newcb, newcb_hbm), (cgrad, cgrad_hbm),
-            )
-        )
-    ]
-    written[0].start()
 
     def weight_half(which, x):
         wg_f[which] = dot_tn(x, dz_all[...])
@@ -305,36 +307,59 @@
         return pair + pltpu.roll(pair, 64, 1)
 
     lax.fori_loop(0, mine // 16, asn_part, 0)
-    as_f[...] = dot(tab_asn[...], featg[...])
+
+    wa.wait_recv()
+    wg_own = wg_f[core] + wg_rx[...].astype(F32)
+    wg_f[core] = wg_own
+    wgb_tx[...] = wg_own.astype(BF16)
+    wrows = wg_own.shape[0]
+    part_rows = wrows // chips
+
+    def wg_rows(step):
+        return pl.ds(pl.multiple_of(((chip + step) % chips) * part_rows, part_rows), part_rows)
+
+    wb = {}
+    for step in range(1, chips):
+        wb[step] = rcopy(
+            wgb_tx.at[wg_rows(step), :], wgb_rx.at[step], wb_s.at[step], wb_r.at[step], (chip_dev(step), y)
+        )
+        wb[step].start()
+
+    as_f[...] = jnp.zeros_like(as_f)
+
+    def code_step(step, carry):
+        code_tile(2 * step, 0)
+        code_tile(2 * step + 1, 0)
+        nodes = pl.ds(pl.multiple_of(step * 256, 256), 256)
+        as_f[...] += dot(tab_asn[:, nodes], featg[nodes, :])
+        return carry
+
+    steps = grp // 256
+    lax.fori_loop(0, steps // 2, code_step, 0)
+    arrived(daggg, d_s, d_r, 0)
+    d_copies[4].start()
+    arrived(daggg, d_s, d_r, 1)
+    d_copies[5].start()
+    lax.fori_loop(steps // 2, steps, code_step, 0)
+
     as_cnt[...] = dot(as_acc[...], jnp.ones((128, 128), BF16))
     as_tx[:, 0:width] = as_f[own_half:, :].astype(BF16)
     as_tx[:, width:] = split_count(as_cnt[own_half:, :])
     aa = rcopy(as_tx, as_rx, aa_s, aa_r, (other, y))
     aa.start()
 
-    tiles = grp // 128
-    lax.fori_loop(0, tiles // 4, code_tile, 0)
-
-    arrived(daggg, d_s, d_r, 0)
-    d_copies[4].start()
-    arrived(daggg, d_s, d_r, 1)
-    d_copies[5].start()
-
-    wa.wait_recv()
-    wg_own = wg_f[core] + wg_rx[...].astype(F32)
-    wg_f[core] = wg_own
-    wgb_tx[...] = wg_own.astype(BF16)
-    part_rows = wg_own.shape[0] // chips
-
-    def wg_rows(step):
-        return pl.ds(pl.multiple_of(((chip + step) % chips) * part_rows, part_rows), part_rows)
-
-    wb = {}
-    for step in range(1, chips):
-        wb[step] = rcopy(
-            wgb_tx.at[wg_rows(step), :], wgb_rx.at[step], wb_s.at[step], wb_r.at[step], (chip_dev(step), y)
-        )
-        wb[step].start()
+    lax.fori_loop(0, grp // 128, ret_tile, 0)
+
+    for step in range(1, chips):
+        wb[step].wait_recv()
+    share = wg_f[core, wg_rows(0), :]
+    for step in range(1, chips):
+        share = share + wgb_rx[step].astype(F32)
+    wgc[0] = share
+    wc = []
+    for at, (peer, slot) in enumerate(((y_right, 3), (y_left, 1), (y_far, 2))):
+        wc.append(rcopy(wgc.at[0], wgc.at[slot], wc_s.at[at], wc_r.at[at], (w, peer)))
+        wc[-1].start()
 
     aa.wait_recv()
     as_f[0:own_half, :] += as_rx[:, 0:width].astype(F32)
@@ -348,26 +373,25 @@
             ab[step] = rcopy(asb_tx.at[step], asb_rx.at[step], ab_s.at[step], ab_r.at[step], (chip_dev(step), y))
             ab[step].start()
 
-    lax.fori_loop(tiles // 4, tiles // 2, code_tile, 0)
-
-    for step in range(1, chips):
-        wb[step].wait_recv()
-    share = wg_f[core, wg_rows(0), :]
-    for step in range(1, chips):
-        share = share + wgb_rx[step].astype(F32)
-    wgc[0] = share
-    wc = []
-    for at, (peer, slot) in enumerate(((y_right, 3), (y_left, 1), (y_far, 2))):
-        wc.append(rcopy(wgc.at[0], wgc.at[slot], wc_s.at[at], wc_r.at[at], (w, peer)))
-        wc[-1].start()
-
-    lax.fori_loop(tiles // 2, tiles, code_tile, 0)
+    arrived(daggg, d_s, d_r, 2)
+    arrived(daggg, d_s, d_r, 3)
+    acc[...] = dot(tab_code[:, 0 : 2 * n], daggg[0 : 2 * n, :]) + dot(tab_code[:, 3 * n :], daggg[3 * n :, :])
+    ret[...] = dot_nt(dz_all[...], ws[...]) + (1.0 / 8) * (
+        dot(tab_ret[:, 0 : 2 * n], daggg[0 : 2 * n, :]) + dot(tab_ret[:, 3 * n :], daggg[3 * n :, :])
+    )
+    arrived(daggg, d_s, d_r, 4)
+    arrived(daggg, d_s, d_r, 5)
+    last = daggg[2 * n : 3 * n, :]
+    cg_tx[...] = ((acc[own_half:, :] + dot(tab_code[own_half:, 2 * n : 3 * n], last)) * (1.0 / 16)).astype(BF16)
+    ca = rcopy(cg_tx, cg_rx, ca_s, ca_r, (other, y))
+    ca.start()
+    acc[0:own_half, :] = (acc[0:own_half, :] + dot(tab_code[0:own_half, 2 * n : 3 * n], last)) * (1.0 / 16)
 
     for at in range(3):
         wc[at].wait_recv()
 
     def share_rows(dev):
-        return pl.ds(pl.multiple_of((dev % 2) * wg_own.shape[0] + (dev // 2) * part_rows, part_rows), part_rows)
+        return pl.ds(pl.multiple_of((dev % 2) * wrows + (dev // 2) * part_rows, part_rows), part_rows)
 
     wgd[share_rows(w), :] = (wgc[0] + wgc[1] + wgc[2] + wgc[3]).astype(BF16)
 
@@ -379,7 +403,15 @@
 
     lax.fori_loop(1, wide, spread, 0)
 
-    lax.fori_loop(0, tiles, ret_tile, 0)
+    ca.wait_recv()
+    cb = {}
+    for step in range(1, chips):
+        rows = pl.ds(step * shard, shard)
+        cgb_tx[step] = (acc[rows, :] + cg_rx[rows, :].astype(F32)).astype(BF16)
+        cb[step] = rcopy(cgb_tx.at[step], cgb_rx.at[step], cb_s.at[step], cb_r.at[step], (chip_dev(step), y))
+        cb[step].start()
+
+    fgrad[...] = (ret[...] + dot(tab_ret[:, 2 * n : 3 * n], last) * (1.0 / 8)).astype(BF16)
 
     own_sum = as_f[0:shard, :]
     own_cnt = as_cnt[0:shard, :]
@@ -401,33 +433,6 @@
     for part in range(width // 128):
         lanes = slice(part * 128, part * 128 + 128)
         newcb[:, lanes] = (decay_rate * old[:, lanes] + (1.0 - decay_rate) * own_sum[:, lanes]) * scale
-    written[4].start()
-
-    ret[...] = dot_nt(dz_all[...], ws[...])
-    acc[...] = dot(tab_code[:, 0:n], daggg[0:n, :])
-    ret[...] += dot(tab_ret[:, 0:n], daggg[0:n, :]) * (1.0 / 8)
-    arrived(daggg, d_s, d_r, 2)
-    acc[...] += dot(tab_code[:, 3 * n : 4 * n], daggg[3 * n : 4 * n, :])
-    ret[...] += dot(tab_ret[:, 3 * n : 4 * n], daggg[3 * n : 4 * n, :]) * (1.0 / 8)
-    arrived(daggg, d_s, d_r, 3)
-    acc[...] += dot(tab_code[:, n : 2 * n], daggg[n : 2 * n, :])
-    ret[...] += dot(tab_ret[:, n : 2 * n], daggg[n : 2 * n, :]) * (1.0 / 8)
-    arrived(daggg, d_s, d_r, 4)
-    arrived(daggg, d_s, d_r, 5)
-    last = daggg[2 * n : 3 * n, :]
-    cg_tx[...] = ((acc[own_half:, :] + dot(tab_code[own_half:, 2 * n : 3 * n], last)) * (1.0 / 16)).astype(BF16)
-    ca = rcopy(cg_tx, cg_rx, ca_s, ca_r, (other, y))
-    ca.start()
-    acc[0:own_half, :] = (acc[0:own_half, :] + dot(tab_code[0:own_half, 2 * n : 3 * n], last)) * (1.0 / 16)
-    fgrad[...] = (ret[...] + dot(tab_ret[:, 2 * n : 3 * n], last) * (1.0 / 8)).astype(BF16)
-    written[1].start()
-    ca.wait_recv()
-    cb = {}
-    for step in range(1, chips):
-        rows = pl.ds(step * shard, shard)
-        cgb_tx[step] = (acc[rows, :] + cg_rx[rows, :].astype(F32)).astype(BF16)
-        cb[step] = rcopy(cgb_tx.at[step], cgb_rx.at[step], cb_s.at[step], cb_r.at[step], (chip_dev(step), y))
-        cb[step].start()
 
     def gathered(step, carry):
         source = (w + wide - step) % wide
@@ -437,18 +442,14 @@
         return carry
 
     lax.fori_loop(1, wide, gathered, 0)
-    wrows = wg_own.shape[0]
-    wgrads[0] = wgd[0:wrows, :].astype(F32)
-    wgrads[1] = wgd[wrows:, :].astype(F32)
-    written[2].start()
-    written[3].start()
+    sgrad[...] = wgd[0:wrows, :].astype(F32)
+    ngrad[...] = wgd[wrows:, :].astype(F32)
 
     own = acc[0:shard, :] + cg_rx[0:shard, :].astype(F32)
     for step in range(1, chips):
         cb[step].wait_recv()
         own = own + cgb_rx[step].astype(F32)
     cgrad[...] = own
-    written[5].start()
 
     for copy in (*f_copies, *d_copies, *i_copies, wa, aa, ca, *wc):
         copy.wait_send()
@@ -464,12 +465,9 @@
         return carry
 
     lax.fori_loop(1, wide, sent, 0)
-    for copy in written:
-        copy.wait()
-
-
-def copy_kernel(*refs):
-    count = len(refs) // 2
+
+
+def copy_kernel(count, *refs):
     copies = [pltpu.make_async_copy(refs[at], refs[count + at], refs[-1].at[at]) for at in range(count)]
     for copy in copies:
         copy.start()
@@ -487,7 +485,7 @@
     shard = codes // (wide * narrow)
     mine = codes // narrow
     grp = n * narrow
-    hbm = pl.BlockSpec(memory_space=pl.ANY)
+    hbm = pl.BlockSpec(memory_space=pltpu.HBM)
     dma = pltpu.SemaphoreType.DMA
     wide_rows = self_weight.shape[0]
     scratch = [
@@ -496,15 +494,11 @@
         pltpu.VMEM((codes // 128, 128), F32),
         pltpu.VMEM(self_weight.shape, BF16),
         pltpu.VMEM(neighbour_weight.shape, BF16),
-        pltpu.VMEM((n, width), BF16),
-        pltpu.VMEM((n, width), BF16),
-        pltpu.VMEM((2, *self_weight.shape), F32),
-        pltpu.VMEM((shard, width), F32),
-        pltpu.VMEM((shard, width), F32),
         pltpu.VMEM((codes, width), BF16),
         pltpu.VMEM((grp, width), BF16),
         pltpu.VMEM((grp, width), BF16),
-        pltpu.VMEM((narrow, IDX_ROWS, n), I32),
+        pltpu.VMEM((IDX_ROWS, n), I32),
+        pltpu.VMEM((narrow, IDX_ROWS, n), jnp.int16),
         pltpu.VMEM((codes, n), BF16),
         pltpu.VMEM((grp, n), BF16),
         pltpu.VMEM((mine, grp), BF16),
@@ -545,7 +539,7 @@
         pltpu.VMEM((chips, shard, width), BF16),
         pltpu.VMEM((chips, shard, width), BF16),
         pltpu.VMEM((128, 128), F32),
-        dma((9,)), dma((6,)),
+        dma((9,)),
         dma((6,)), dma((6,)), dma((6,)), dma((6,)), dma((3,)), dma((3,)),
         dma, dma, dma((chips,)), dma((chips,)), dma((3,)), dma((3,)), dma((wide,)), dma((wide,)),
         dma, dma, dma((chips,)), dma((chips,)), dma, dma, dma((chips,)), dma((chips,)),
@@ -558,26 +552,28 @@
         jax.ShapeDtypeStruct((shard, width), F32),
         jax.ShapeDtypeStruct((shard, width), F32),
     )
-    results = pl.pallas_call(
-        functools.partial(kernel, wide, narrow, shard),
-        out_shape=shapes,
-        in_specs=[hbm] * 9,
-        out_specs=(hbm,) * 6,
-        scratch_shapes=scratch,
-        compiler_params=pltpu.CompilerParams(
-            collective_id=0, has_side_effects=True, vmem_limit_bytes=58 * 1024 * 1024
-        ),
-    )(
+    vm = pl.BlockSpec(memory_space=pltpu.VMEM)
+    operands = (
         features, neighbours.T, code_ids.T, assignment.reshape(1, n), cotangent,
         code_sums, code_counts.reshape(codes // 128, 128), self_weight, neighbour_weight,
     )
+    results = pl.pallas_call(
+        functools.partial(kernel, wide, narrow, shard),
+        out_shape=tuple(pltpu.VMEM(shape.shape, shape.dtype) for shape in shapes),
+        in_specs=[hbm] * 9,
+        out_specs=(vm,) * 6,
+        scratch_shapes=scratch,
+        compiler_params=pltpu.CompilerParams(
+            collective_id=0, has_side_effects=True, vmem_limit_bytes=48 * 1024 * 1024
+        ),
+    )(*(pltpu.with_memory_space_constraint(operand, pltpu.HBM) for operand in operands))
     return pl.pallas_call(
-        copy_kernel,
+        functools.partial(copy_kernel, len(shapes)),
         out_shape=shapes,
-        in_specs=[hbm] * 6,
+        in_specs=[vm] * 6,
         out_specs=(hbm,) * 6,
         scratch_shapes=[dma((6,))],
-        compiler_params=pltpu.CompilerParams(vmem_limit_bytes=62 * 1024 * 1024),
+        compiler_params=pltpu.CompilerParams(vmem_limit_bytes=8 * 1024 * 1024),
     )(*results)
 
 

time: 90.7 us -> 48.9 us (0.54)
  Pallas kernels: 90 us -> 48.2 us
    pallas_call x1, Pallas kernels: 34.9 us -> 1.03 us  [on_device(): pl.pallas_call(functools.partial(copy_kernel, len(shapes)), out_shape=sha...]
    pallas_call x1, Pallas kernels: 55 us -> 47.1 us  [on_device(): pl.pallas_call(functools.partial(kernel, wide, narrow, shard), out_shape=...]
where the time goes in v3:
time: 48.9 us; the launch traced here: 48.8 us
  Pallas kernels  48.2 us (99%)
  between operations  0.64 us (1%)
    pallas_call x1, Pallas kernels, on_device(): pl.pallas_call(functools.partial(kernel, wide, narrow, shard), out_shape=...  47.1 us
    pallas_call x1, Pallas kernels, on_device(): pl.pallas_call(functools.partial(copy_kernel, len(shapes)), out_shape=sha...  1.03 us

profile of v3, /device:TPU:1, one launch (start us, length us, event | category | flops | bytes accessed | tf_op | source)
XLA Modules:
  0.0 48.8 jit_solution(6246853870498290087)
XLA Ops:
  0.6 47.1 %shard_map.136 = (bf16[512,256]{1,0:T(8,128)(2,1)S(1)}, bf16[512,256]{1,0:T(8,128)(2,1)S(1)}, f32[256,256]{1,0:T(8,128)S(1)}, f32[256,256]{1,0:T(8,128)S(1)}, f3...) custom-call(bf16[512,256]{1,0:T(8,128)(2,1)} %feat_hbm.1, s32[8,512]{1,0:T(8,128)} %bitcast.5, s32[16,512]{1,0:T(8,128)} %bitcast.4, ...), custom_call_target="tpu_custom_call" | custom-call | tf_op jit(solution)/shard_map/pallas_call | solution.py:560
  47.8 1.0 %shard_map.137 = (bf16[512,256]{1,0:T(8,128)(2,1)}, bf16[512,256]{1,0:T(8,128)(2,1)}, f32[256,256]{1,0:T(8,128)}, f32[256,256]{1,0:T(8,128)}, f32[32,256]{1,0:T(8,128)}, /*index=5*/f32[32,256]{1,0:T(8,128)}) custom-call(bf16[512,256]{1,0:T(8,128)(2,1)S(1)} %get-tuple-element.12.refs_0_, bf16[512,256]{1,0:T(8,128)(2,1)S(1)} %get-tuple-element.13.refs_1_, ...), custom_call_target="tpu_custom_call" | custom-call | tf_op jit(solution)/shard_map/pallas_call | solution.py:570

commit v4 on v3

--- a/solution.py
+++ b/solution.py
@@ -58,10 +58,10 @@
     out, fgrad, sgrad, ngrad, newcb, cgrad,
     cot, sums, counts, ws, wn,
     codebook, featg, daggg, idx_own, idxg, tab_far, tab_near, tab_code, tab_ret, tab_asn,
-    hi_f, val_f, hi_n, val_n, hi_t, val_t, hi_r, val_r, row_a, far, near, hid, dz_all, agg_all, acc, ret,
+    hi_f, val_f, hi_n, val_n, hi_t, val_t, hi_r, val_r, row_a, far, near, hid, dz_all, agg_all, acc,
     wg_f, wg_tx, wg_rx, wgb_tx, wgb_rx, wgc, wgd, as_f, as_cnt, as_acc, as_tx, as_rx, asb_tx, asb_rx,
     cg_tx, cg_rx, cgb_tx, cgb_rx, cnt_col,
-    in_sem, f_s, f_r, d_s, d_r, i_s, i_r, wa_s, wa_r, wb_s, wb_r, wc_s, wc_r, wd_s, wd_r,
+    in_sem, f_s, f_r, d_s, d_r, i_s, i_r, wa_s, wa_r, wb_s, wb_r, wc_s, wc_r, wd_s, wd_r, we_s, we_r,
     aa_s, aa_r, ab_s, ab_r, ca_s, ca_r, cb_s, cb_r,
 ):
     n = cot.shape[0]
@@ -78,8 +78,24 @@
     y_right, y_left, y_far = (y + 1) % narrow, (y + 3) % narrow, (y + 2) % narrow
     other = chip * 2 + (1 - core)
 
+    x_chips = min(4, chips)
+    z_chips = chips // x_chips
+    chip_z, chip_x = chip // x_chips, chip % x_chips
+
+    def chip_at(step, sign=1):
+        step_z, step_x = step // x_chips, step % x_chips
+        at_z = (chip_z + (step_z if sign > 0 else z_chips - step_z)) % z_chips
+        at_x = (chip_x + (step_x if sign > 0 else x_chips - step_x)) % x_chips
+        return at_z * x_chips + at_x
+
     def chip_dev(step):
-        return ((chip + step) % chips) * 2 + core
+        return chip_at(step) * 2 + core
+
+    def hops(step):
+        step_z, step_x = step // x_chips, step % x_chips
+        return min(step_z, z_chips - step_z) + min(step_x, x_chips - step_x)
+
+    steps_out = sorted(range(1, chips), key=lambda step: -hops(step))
 
     def rcopy(src, dst, ssem, rsem, dev):
         return pltpu.make_async_remote_copy(
@@ -111,14 +127,11 @@
     for peer in (y_right, y_left, y_far):
         pl.semaphore_signal(barrier, inc=1, device_id=(w, peer), device_id_type=MESH)
 
-    def greet(step, carry):
-        pl.semaphore_signal(barrier, inc=1, device_id=((w + step) % wide, y), device_id_type=MESH)
-        return carry
-
-    lax.fori_loop(1, wide, greet, 0)
+    for peer in (*(chip_dev(step) for step in steps_out), other):
+        pl.semaphore_signal(barrier, inc=1, device_id=(peer, y), device_id_type=MESH)
     for at in range(4):
         fetched[at].wait()
-    pl.semaphore_wait(barrier, narrow - 1 + wide - 1)
+    pl.semaphore_wait(barrier, narrow - 1 + chips)
 
     def low(slot):
         return pl.ds(slot * n, half)
@@ -262,19 +275,22 @@
 
     def place(k):
         kw = k >> (shard_bits + narrow_bits)
-        row = ((((kw & 1) ^ core) * chips + (((kw >> 1) - chip) & (chips - 1))) << shard_bits) | (k & (shard - 1))
+        kc = kw >> 1
+        step = ((((kc >> (x_chips.bit_length() - 1)) - chip_z) & (z_chips - 1)) * x_chips) | ((kc - chip_x) & (x_chips - 1))
+        row = ((((kw & 1) ^ core) * chips + step) << shard_bits) | (k & (shard - 1))
         return row, ((k >> shard_bits) & (narrow - 1)) == y
 
     for slot in range(narrow):
         lanes = pl.ds(slot * n, n)
-        ids = idxg[slot, 0:8, :]
+        block = idxg[slot].astype(I32)
+        ids = block[0:8, :]
         hi_r[:, lanes] = ids & (ret_spots - 1)
         local = ids & (n - 1)
         val_r[:, lanes] = jnp.where((ids >> node_bits) == y, jnp.int32(1) << ((local >> ret_bits) * 4), 0)
-        row, hit = place(idxg[slot, 8:24, :])
+        row, hit = place(block[8:24, :])
         hi_t[:, lanes] = row & (mine_spots - 1)
         val_t[:, lanes] = jnp.where(hit, jnp.int32(1) << ((row >> mine_bits) * 4), 0)
-        row, hit = place(idxg[slot, 24:32, :])
+        row, hit = place(block[24:32, :])
         row_a[:, lanes] = jnp.where(hit, row, -1)
 
     def asn_part(part, carry):
@@ -306,7 +322,7 @@
         pair = pair.astype(F32)
         return pair + pltpu.roll(pair, 64, 1)
 
-    lax.fori_loop(0, mine // 16, asn_part, 0)
+    lax.fori_loop(0, mine // 64, asn_part, 0)
 
     wa.wait_recv()
     wg_own = wg_f[core] + wg_rx[...].astype(F32)
@@ -315,15 +331,16 @@
     wrows = wg_own.shape[0]
     part_rows = wrows // chips
 
-    def wg_rows(step):
-        return pl.ds(pl.multiple_of(((chip + step) % chips) * part_rows, part_rows), part_rows)
+    def wg_rows(at):
+        return pl.ds(pl.multiple_of(at * part_rows, part_rows), part_rows)
 
     wb = {}
-    for step in range(1, chips):
+    for step in steps_out:
         wb[step] = rcopy(
-            wgb_tx.at[wg_rows(step), :], wgb_rx.at[step], wb_s.at[step], wb_r.at[step], (chip_dev(step), y)
+            wgb_tx.at[wg_rows(chip_at(step)), :], wgb_rx.at[step], wb_s.at[step], wb_r.at[step], (chip_dev(step), y)
         )
         wb[step].start()
+    lax.fori_loop(mine // 64, mine // 16, asn_part, 0)
 
     as_f[...] = jnp.zeros_like(as_f)
 
@@ -348,12 +365,10 @@
     aa = rcopy(as_tx, as_rx, aa_s, aa_r, (other, y))
     aa.start()
 
-    lax.fori_loop(0, grp // 128, ret_tile, 0)
-
-    for step in range(1, chips):
+    for step in steps_out:
         wb[step].wait_recv()
-    share = wg_f[core, wg_rows(0), :]
-    for step in range(1, chips):
+    share = wg_f[core, wg_rows(chip), :]
+    for step in steps_out:
         share = share + wgb_rx[step].astype(F32)
     wgc[0] = share
     wc = []
@@ -365,57 +380,65 @@
     as_f[0:own_half, :] += as_rx[:, 0:width].astype(F32)
     as_cnt[0:own_half, :] += join_count(as_rx[:, width:])
     ab = {}
-    for step in range(chips):
+    for step in steps_out:
         rows = pl.ds(step * shard, shard)
         asb_tx[step, :, 0:width] = as_f[rows, :].astype(BF16)
         asb_tx[step, :, width:] = split_count(as_cnt[rows, :])
-        if step:
-            ab[step] = rcopy(asb_tx.at[step], asb_rx.at[step], ab_s.at[step], ab_r.at[step], (chip_dev(step), y))
-            ab[step].start()
-
+        ab[step] = rcopy(asb_tx.at[step], asb_rx.at[step], ab_s.at[step], ab_r.at[step], (chip_dev(step), y))
+        ab[step].start()
+
+    acc[...] = dot(tab_code[:, 0:n], daggg[0:n, :])
     arrived(daggg, d_s, d_r, 2)
     arrived(daggg, d_s, d_r, 3)
-    acc[...] = dot(tab_code[:, 0 : 2 * n], daggg[0 : 2 * n, :]) + dot(tab_code[:, 3 * n :], daggg[3 * n :, :])
-    ret[...] = dot_nt(dz_all[...], ws[...]) + (1.0 / 8) * (
-        dot(tab_ret[:, 0 : 2 * n], daggg[0 : 2 * n, :]) + dot(tab_ret[:, 3 * n :], daggg[3 * n :, :])
-    )
+    acc[...] += dot(tab_code[:, n : 2 * n], daggg[n : 2 * n, :]) + dot(tab_code[:, 3 * n :], daggg[3 * n :, :])
     arrived(daggg, d_s, d_r, 4)
     arrived(daggg, d_s, d_r, 5)
     last = daggg[2 * n : 3 * n, :]
-    cg_tx[...] = ((acc[own_half:, :] + dot(tab_code[own_half:, 2 * n : 3 * n], last)) * (1.0 / 16)).astype(BF16)
-    ca = rcopy(cg_tx, cg_rx, ca_s, ca_r, (other, y))
-    ca.start()
-    acc[0:own_half, :] = (acc[0:own_half, :] + dot(tab_code[0:own_half, 2 * n : 3 * n], last)) * (1.0 / 16)
+    block = own_half // 2
+
+    def finished(first):
+        rows = slice(first, first + block)
+        return (acc[rows, :] + dot(tab_code[rows, 2 * n : 3 * n], last)) * (1.0 / 16)
+
+    ca = {}
+    for part in (1, 0):
+        rows = pl.ds(part * block, block)
+        cg_tx[rows, :] = finished(own_half + part * block).astype(BF16)
+        ca[part] = rcopy(cg_tx.at[rows, :], cg_rx.at[rows, :], ca_s.at[part], ca_r.at[part], (other, y))
+        ca[part].start()
+    for part in (1, 0):
+        acc[part * block : part * block + block, :] = finished(part * block)
 
     for at in range(3):
         wc[at].wait_recv()
 
-    def share_rows(dev):
-        return pl.ds(pl.multiple_of((dev % 2) * wrows + (dev // 2) * part_rows, part_rows), part_rows)
-
-    wgd[share_rows(w), :] = (wgc[0] + wgc[1] + wgc[2] + wgc[3]).astype(BF16)
-
-    def spread(step, carry):
-        rcopy(
-            wgd.at[share_rows(w), :], wgd.at[share_rows(w), :], wd_s.at[step], wd_r.at[step], ((w + step) % wide, y)
-        ).start()
-        return carry
-
-    lax.fori_loop(1, wide, spread, 0)
-
-    ca.wait_recv()
+    def share_rows(at):
+        return pl.ds(pl.multiple_of(core * wrows + at * part_rows, part_rows), part_rows)
+
+    wgd[share_rows(chip), :] = (wgc[0] + wgc[1] + wgc[2] + wgc[3]).astype(BF16)
+    wd = {}
+    for step in steps_out:
+        mine_rows = wgd.at[share_rows(chip), :]
+        wd[step] = rcopy(mine_rows, mine_rows, wd_s.at[step], wd_r.at[step], (chip_dev(step), y))
+        wd[step].start()
+
     cb = {}
-    for step in range(1, chips):
-        rows = pl.ds(step * shard, shard)
-        cgb_tx[step] = (acc[rows, :] + cg_rx[rows, :].astype(F32)).astype(BF16)
-        cb[step] = rcopy(cgb_tx.at[step], cgb_rx.at[step], cb_s.at[step], cb_r.at[step], (chip_dev(step), y))
-        cb[step].start()
-
-    fgrad[...] = (ret[...] + dot(tab_ret[:, 2 * n : 3 * n], last) * (1.0 / 8)).astype(BF16)
+    for part in (1, 0):
+        ca[part].wait_recv()
+        for step in steps_out:
+            if step * shard // block != part:
+                continue
+            rows = pl.ds(step * shard, shard)
+            cgb_tx[step] = (acc[rows, :] + cg_rx[rows, :].astype(F32)).astype(BF16)
+            cb[step] = rcopy(cgb_tx.at[step], cgb_rx.at[step], cb_s.at[step], cb_r.at[step], (chip_dev(step), y))
+            cb[step].start()
+
+    lax.fori_loop(0, grp // 128, ret_tile, 0)
+    fgrad[...] = (dot_nt(dz_all[...], ws[...]) + dot(tab_ret[...], daggg[...]) * (1.0 / 8)).astype(BF16)
 
     own_sum = as_f[0:shard, :]
     own_cnt = as_cnt[0:shard, :]
-    for step in range(1, chips):
+    for step in steps_out:
         ab[step].wait_recv()
         own_sum = own_sum + asb_rx[step, :, 0:width].astype(F32)
         own_cnt = own_cnt + join_count(asb_rx[step, :, width:])
@@ -434,37 +457,28 @@
         lanes = slice(part * 128, part * 128 + 128)
         newcb[:, lanes] = (decay_rate * old[:, lanes] + (1.0 - decay_rate) * own_sum[:, lanes]) * scale
 
-    def gathered(step, carry):
-        source = (w + wide - step) % wide
-        rcopy(
-            wgd.at[share_rows(source), :], wgd.at[share_rows(source), :], wd_s.at[step], wd_r.at[step], (source, y)
-        ).wait_recv()
-        return carry
-
-    lax.fori_loop(1, wide, gathered, 0)
+    for step in steps_out:
+        source = wgd.at[share_rows(chip_at(step, -1)), :]
+        rcopy(source, source, wd_s.at[step], wd_r.at[step], (chip_dev(step), y)).wait_recv()
+    own_rows = wgd.at[pl.ds(pl.multiple_of(core * wrows, wrows), wrows), :]
+    other_rows = wgd.at[pl.ds(pl.multiple_of((1 - core) * wrows, wrows), wrows), :]
+    we = rcopy(own_rows, own_rows, we_s, we_r, (other, y))
+    we.start()
+    rcopy(other_rows, other_rows, we_s, we_r, (other, y)).wait_recv()
     sgrad[...] = wgd[0:wrows, :].astype(F32)
     ngrad[...] = wgd[wrows:, :].astype(F32)
 
     own = acc[0:shard, :] + cg_rx[0:shard, :].astype(F32)
-    for step in range(1, chips):
+    for step in steps_out:
         cb[step].wait_recv()
         own = own + cgb_rx[step].astype(F32)
     cgrad[...] = own
 
-    for copy in (*f_copies, *d_copies, *i_copies, wa, aa, ca, *wc):
+    for copy in (*f_copies, *d_copies, *i_copies, wa, aa, *ca.values(), *wc, we):
         copy.wait_send()
-    for step in range(1, chips):
-        wb[step].wait_send()
-        ab[step].wait_send()
-        cb[step].wait_send()
-
-    def sent(step, carry):
-        rcopy(
-            wgd.at[share_rows(w), :], wgd.at[share_rows(w), :], wd_s.at[step], wd_r.at[step], ((w + step) % wide, y)
-        ).wait_send()
-        return carry
-
-    lax.fori_loop(1, wide, sent, 0)
+    for step in steps_out:
+        for copies in (wb, ab, wd, cb):
+            copies[step].wait_send()
 
 
 def copy_kernel(count, *refs):
@@ -519,7 +533,6 @@
         pltpu.VMEM((n, width), BF16),
         pltpu.VMEM((n, width), BF16),
         pltpu.VMEM((mine, width), F32),
-        pltpu.VMEM((n, width), F32),
         pltpu.VMEM((2, wide_rows, width), F32),
         pltpu.VMEM((wide_rows, width), BF16),
         pltpu.VMEM((wide_rows, width), BF16),
@@ -541,8 +554,8 @@
         pltpu.VMEM((128, 128), F32),
         dma((9,)),
         dma((6,)), dma((6,)), dma((6,)), dma((6,)), dma((3,)), dma((3,)),
-        dma, dma, dma((chips,)), dma((chips,)), dma((3,)), dma((3,)), dma((wide,)), dma((wide,)),
-        dma, dma, dma((chips,)), dma((chips,)), dma, dma, dma((chips,)), dma((chips,)),
+        dma, dma, dma((chips,)), dma((chips,)), dma((3,)), dma((3,)), dma((chips,)), dma((chips,)), dma, dma,
+        dma, dma, dma((chips,)), dma((chips,)), dma((2,)), dma((2,)), dma((chips,)), dma((chips,)),
     ]
     shapes = (
         jax.ShapeDtypeStruct((n, width), BF16),

time: 48.9 us -> 47.2 us (0.965)
  Pallas kernels: 48.2 us -> 46.5 us
    pallas_call x1, Pallas kernels: 47.1 us -> 45.5 us  [on_device(): pl.pallas_call(functools.partial(kernel, wide, narrow, shard), out_shape=...]
where the time goes in v4:
time: 47.2 us; the launch traced here: 47.1 us
  Pallas kernels  46.5 us (99%)
  between operations  0.64 us (1%)
    pallas_call x1, Pallas kernels, on_device(): pl.pallas_call(functools.partial(kernel, wide, narrow, shard), out_shape=...  45.5 us
    pallas_call x1, Pallas kernels, on_device(): pl.pallas_call(functools.partial(copy_kernel, len(shapes)), out_shape=sha...  1.03 us

profile of v4, /device:TPU:1, one launch (start us, length us, event | category | flops | bytes accessed | tf_op | source)
XLA Modules:
  0.0 47.1 jit_solution(17545259139754711022)
XLA Ops:
  0.6 45.5 %shard_map.136 = (bf16[512,256]{1,0:T(8,128)(2,1)S(1)}, bf16[512,256]{1,0:T(8,128)(2,1)S(1)}, f32[256,256]{1,0:T(8,128)S(1)}, f32[256,256]{1,0:T(8,128)S(1)}, f3...) custom-call(bf16[512,256]{1,0:T(8,128)(2,1)} %feat_hbm.1, s32[8,512]{1,0:T(8,128)} %bitcast.5, s32[16,512]{1,0:T(8,128)} %bitcast.4, ...), custom_call_target="tpu_custom_call" | custom-call | tf_op jit(solution)/shard_map/pallas_call | solution.py:573
  46.1 1.0 %shard_map.137 = (bf16[512,256]{1,0:T(8,128)(2,1)}, bf16[512,256]{1,0:T(8,128)(2,1)}, f32[256,256]{1,0:T(8,128)}, f32[256,256]{1,0:T(8,128)}, f32[32,256]{1,0:T(8,128)}, /*index=5*/f32[32,256]{1,0:T(8,128)}) custom-call(bf16[512,256]{1,0:T(8,128)(2,1)S(1)} %get-tuple-element.12.refs_0_, bf16[512,256]{1,0:T(8,128)(2,1)S(1)} %get-tuple-element.13.refs_1_, ...), custom_call_target="tpu_custom_call" | custom-call | tf_op jit(solution)/shard_map/pallas_call | solution.py:583

commit v5 on v4

--- a/solution.py
+++ b/solution.py
@@ -58,7 +58,7 @@
     out, fgrad, sgrad, ngrad, newcb, cgrad,
     cot, sums, counts, ws, wn,
     codebook, featg, daggg, idx_own, idxg, tab_far, tab_near, tab_code, tab_ret, tab_asn,
-    hi_f, val_f, hi_n, val_n, hi_t, val_t, hi_r, val_r, row_a, far, near, hid, dz_all, agg_all, acc,
+    hi_f, val_f, hi_n, val_n, hi_t, val_t, hi_r, val_r, row_a, asn_hi, asn_lo, far, near, hid, dz_all, taken, acc,
     wg_f, wg_tx, wg_rx, wgb_tx, wgb_rx, wgc, wgd, as_f, as_cnt, as_acc, as_tx, as_rx, asb_tx, asb_rx,
     cg_tx, cg_rx, cgb_tx, cgb_rx, cnt_col,
     in_sem, f_s, f_r, d_s, d_r, i_s, i_r, wa_s, wa_r, wb_s, wb_r, wc_s, wc_r, wd_s, wd_r, we_s, we_r,
@@ -202,14 +202,7 @@
         return carry
 
     far_tiles = (n // 128) * (far_spots // 128)
-    lax.fori_loop(0, far_tiles // 2, far_tile, 0)
-    arrived(featg, f_s, f_r, 0)
-    f_copies[4].start()
-    arrived(featg, f_s, f_r, 1)
-    f_copies[5].start()
-    for copy in i_copies:
-        copy.start()
-    lax.fori_loop(far_tiles // 2, far_tiles, far_tile, 0)
+    lax.fori_loop(0, far_tiles, far_tile, 0)
     width = sums.shape[1]
     for at in range(4, 9):
         fetched[at].wait()
@@ -221,6 +214,12 @@
             at = (slice(block * 128, block * 128 + 128), slice(part * 128, part * 128 + 128))
             codebook[at] = (sums[at] * column).astype(BF16)
     far[...] = jnp.zeros_like(far)
+    arrived(featg, f_s, f_r, 0)
+    f_copies[4].start()
+    arrived(featg, f_s, f_r, 1)
+    f_copies[5].start()
+    for copy in i_copies:
+        copy.start()
     near_tiles = (n // 128) * (near_spots // 128)
     step_codes = codes // near_tiles
 
@@ -232,6 +231,7 @@
 
     lax.fori_loop(0, near_tiles, near_step, 0)
     hid[...] = dot(feat[...], ws[...])
+    taken[:, 0:width] = feat[...]
     near[...] = dot_tn(tab_near[0:n, :], feat[...])
     arrived(featg, f_s, f_r, 2)
     near[...] += dot_tn(tab_near[3 * n : 4 * n, :], featg[3 * n : 4 * n, :])
@@ -245,7 +245,7 @@
         rows = pl.ds(at * half, half)
         total = near[rows, :] + dot_tn(tab_near[2 * n : 3 * n, at * half : at * half + half], featg[2 * n : 3 * n, :])
         agg = (total * (1.0 / 8) + far[rows, :] * (1.0 / 16)).astype(BF16)
-        agg_all[rows, :] = agg
+        taken[rows, width:] = agg
         z = hid[rows, :] + dot(agg, wn[...])
         s = jax.nn.sigmoid(z)
         out[rows, :] = (z * s).astype(BF16)
@@ -255,11 +255,10 @@
         d_copies[(0, 1)[at]].start()
         d_copies[(3, 2)[at]].start()
 
-    def weight_half(which, x):
-        wg_f[which] = dot_tn(x, dz_all[...])
-
-    weight_half(0, feat[...])
-    weight_half(1, agg_all[...])
+    wrows = ws.shape[0]
+    local = dot_tn(taken[...], dz_all[...])
+    wg_f[0] = local[0:wrows, :]
+    wg_f[1] = local[wrows:, :]
     wg_tx[...] = wg_f[1 - core].astype(BF16)
     wa = rcopy(wg_tx, wg_rx, wa_s, wa_r, (other, y))
     wa.start()
@@ -293,16 +292,22 @@
         row, hit = place(block[24:32, :])
         row_a[:, lanes] = jnp.where(hit, row, -1)
 
-    def asn_part(part, carry):
-        rows = pl.ds(pl.multiple_of(part * 16, 16), 16)
-        spots = lax.broadcasted_iota(I32, (16, 128), 0) + part * 16
-        total = None
+    all_rows = row_a[0:1, :]
+    asn_hi[...] = jnp.where(lax.broadcasted_iota(I32, asn_hi.shape, 0) == (all_rows >> 4), 1.0, 0.0)
+    asn_lo[...] = jnp.where(lax.broadcasted_iota(I32, (16, grp), 0) == (all_rows & 15), 1.0, 0.0).astype(BF16)
+
+    def asn_part(group, carry):
+        totals = [None] * 8
         for tile in range(grp // 128):
             lanes = slice(tile * 128, tile * 128 + 128)
-            hit = jnp.where(jnp.broadcast_to(row_a[0:1, lanes], (16, 128)) == spots, 1.0, 0.0)
-            tab_asn[rows, lanes] = hit.astype(BF16)
-            total = hit if total is None else total + hit
-        as_acc[rows, :] = total.astype(BF16)
+            fits = asn_hi[pl.ds(pl.multiple_of(group * 8, 8), 8), lanes]
+            low = asn_lo[:, lanes]
+            for part in range(8):
+                hit = jnp.broadcast_to(fits[part : part + 1, :], (16, 128)).astype(BF16) * low
+                tab_asn[pl.ds(pl.multiple_of(group * 128 + part * 16, 16), 16), lanes] = hit
+                totals[part] = hit if tile == 0 else totals[part] + hit
+        for part in range(8):
+            as_acc[pl.ds(pl.multiple_of(group * 128 + part * 16, 16), 16), :] = totals[part]
         return carry
 
     def code_tile(tile, carry):
@@ -322,13 +327,12 @@
         pair = pair.astype(F32)
         return pair + pltpu.roll(pair, 64, 1)
 
-    lax.fori_loop(0, mine // 64, asn_part, 0)
+    lax.fori_loop(0, mine // 512, asn_part, 0)
 
     wa.wait_recv()
     wg_own = wg_f[core] + wg_rx[...].astype(F32)
     wg_f[core] = wg_own
     wgb_tx[...] = wg_own.astype(BF16)
-    wrows = wg_own.shape[0]
     part_rows = wrows // chips
 
     def wg_rows(at):
@@ -340,7 +344,7 @@
             wgb_tx.at[wg_rows(chip_at(step)), :], wgb_rx.at[step], wb_s.at[step], wb_r.at[step], (chip_dev(step), y)
         )
         wb[step].start()
-    lax.fori_loop(mine // 64, mine // 16, asn_part, 0)
+    lax.fori_loop(mine // 512, mine // 128, asn_part, 0)
 
     as_f[...] = jnp.zeros_like(as_f)
 
@@ -387,10 +391,9 @@
         ab[step] = rcopy(asb_tx.at[step], asb_rx.at[step], ab_s.at[step], ab_r.at[step], (chip_dev(step), y))
         ab[step].start()
 
-    acc[...] = dot(tab_code[:, 0:n], daggg[0:n, :])
     arrived(daggg, d_s, d_r, 2)
     arrived(daggg, d_s, d_r, 3)
-    acc[...] += dot(tab_code[:, n : 2 * n], daggg[n : 2 * n, :]) + dot(tab_code[:, 3 * n :], daggg[3 * n :, :])
+    acc[...] = dot(tab_code[:, 0 : 2 * n], daggg[0 : 2 * n, :]) + dot(tab_code[:, 3 * n :], daggg[3 * n :, :])
     arrived(daggg, d_s, d_r, 4)
     arrived(daggg, d_s, d_r, 5)
     last = daggg[2 * n : 3 * n, :]
@@ -527,11 +530,13 @@
         pltpu.VMEM((8, grp), I32),
         pltpu.VMEM((8, grp), I32),
         pltpu.VMEM((8, grp), I32),
+        pltpu.VMEM((mine // 16, grp), F32),
+        pltpu.VMEM((16, grp), BF16),
         pltpu.VMEM((n, width), F32),
         pltpu.VMEM((n, width), F32),
         pltpu.VMEM((n, width), F32),
         pltpu.VMEM((n, width), BF16),
-        pltpu.VMEM((n, width), BF16),
+        pltpu.VMEM((n, 2 * width), BF16),
         pltpu.VMEM((mine, width), F32),
         pltpu.VMEM((2, wide_rows, width), F32),
         pltpu.VMEM((wide_rows, width), BF16),

time: 47.2 us -> 45.6 us (0.966)
  Pallas kernels: 46.5 us -> 44.8 us
    pallas_call x1, Pallas kernels: 45.5 us -> 43.8 us  [on_device(): pl.pallas_call(functools.partial(kernel, wide, narrow, shard), out_shape=...]
where the time goes in v5:
time: 45.6 us; the launch traced here: 45.5 us
  Pallas kernels  44.8 us (98%)
  between operations  0.64 us (1%)
    pallas_call x1, Pallas kernels, on_device(): pl.pallas_call(functools.partial(kernel, wide, narrow, shard), out_shape=...  43.8 us
    pallas_call x1, Pallas kernels, on_device(): pl.pallas_call(functools.partial(copy_kernel, len(shapes)), out_shape=sha...  1.03 us

profile of v5, /device:TPU:1, one launch (start us, length us, event | category | flops | bytes accessed | tf_op | source)
XLA Modules:
  0.0 45.5 jit_solution(17976904533491186314)
XLA Ops:
  0.6 43.8 %shard_map.136 = (bf16[512,256]{1,0:T(8,128)(2,1)S(1)}, bf16[512,256]{1,0:T(8,128)(2,1)S(1)}, f32[256,256]{1,0:T(8,128)S(1)}, f32[256,256]{1,0:T(8,128)S(1)}, f3...) custom-call(bf16[512,256]{1,0:T(8,128)(2,1)} %feat_hbm.1, s32[8,512]{1,0:T(8,128)} %bitcast.5, s32[16,512]{1,0:T(8,128)} %bitcast.4, ...), custom_call_target="tpu_custom_call" | custom-call | tf_op jit(solution)/shard_map/pallas_call | solution.py:578
  44.4 1.0 %shard_map.137 = (bf16[512,256]{1,0:T(8,128)(2,1)}, bf16[512,256]{1,0:T(8,128)(2,1)}, f32[256,256]{1,0:T(8,128)}, f32[256,256]{1,0:T(8,128)}, f32[32,256]{1,0:T(8,128)}, /*index=5*/f32[32,256]{1,0:T(8,128)}) custom-call(bf16[512,256]{1,0:T(8,128)(2,1)S(1)} %get-tuple-element.12.refs_0_, bf16[512,256]{1,0:T(8,128)(2,1)S(1)} %get-tuple-element.13.refs_1_, ...), custom_call_target="tpu_custom_call" | custom-call | tf_op jit(solution)/shard_map/pallas_call | solution.py:588

commit v6 on v5

--- a/solution.py
+++ b/solution.py
@@ -230,6 +230,12 @@
         return carry
 
     lax.fori_loop(0, near_tiles, near_step, 0)
+    for kw in range(wide):
+        kc = kw // 2
+        step = ((kc // x_chips + z_chips - chip_z) % z_chips) * x_chips + (kc % x_chips + x_chips - chip_x) % x_chips
+        to = ((kw + core) % 2) * own_half + step * shard
+        rows = pl.ds(pl.multiple_of((kw * narrow + y) * shard, shard), shard)
+        tab_code[pl.ds(pl.multiple_of(to, shard), shard), 0:n] = tab_far[rows, :]
     hid[...] = dot(feat[...], ws[...])
     taken[:, 0:width] = feat[...]
     near[...] = dot_tn(tab_near[0:n, :], feat[...])
@@ -327,7 +333,17 @@
         pair = pair.astype(F32)
         return pair + pltpu.roll(pair, 64, 1)
 
-    lax.fori_loop(0, mine // 512, asn_part, 0)
+    def assigned(first):
+        rows = pl.ds(first, own_half)
+        lax.fori_loop(first // 128, (first + own_half) // 128, asn_part, 0)
+        as_f[rows, :] = dot(tab_asn[rows, :], featg[...])
+        as_cnt[rows, :] = dot(as_acc[rows, :], jnp.ones((128, 128), BF16))
+
+    assigned(own_half)
+    as_tx[:, 0:width] = as_f[own_half:, :].astype(BF16)
+    as_tx[:, width:] = split_count(as_cnt[own_half:, :])
+    aa = rcopy(as_tx, as_rx, aa_s, aa_r, (other, y))
+    aa.start()
 
     wa.wait_recv()
     wg_own = wg_f[core] + wg_rx[...].astype(F32)
@@ -344,30 +360,27 @@
             wgb_tx.at[wg_rows(chip_at(step)), :], wgb_rx.at[step], wb_s.at[step], wb_r.at[step], (chip_dev(step), y)
         )
         wb[step].start()
-    lax.fori_loop(mine // 512, mine // 128, asn_part, 0)
-
-    as_f[...] = jnp.zeros_like(as_f)
-
-    def code_step(step, carry):
-        code_tile(2 * step, 0)
-        code_tile(2 * step + 1, 0)
-        nodes = pl.ds(pl.multiple_of(step * 256, 256), 256)
-        as_f[...] += dot(tab_asn[:, nodes], featg[nodes, :])
-        return carry
-
-    steps = grp // 256
-    lax.fori_loop(0, steps // 2, code_step, 0)
+    assigned(0)
+
+    aa.wait_recv()
+    as_f[0:own_half, :] += as_rx[:, 0:width].astype(F32)
+    as_cnt[0:own_half, :] += join_count(as_rx[:, width:])
+    ab = {}
+    for step in steps_out:
+        rows = pl.ds(step * shard, shard)
+        asb_tx[step, :, 0:width] = as_f[rows, :].astype(BF16)
+        asb_tx[step, :, width:] = split_count(as_cnt[rows, :])
+        ab[step] = rcopy(asb_tx.at[step], asb_rx.at[step], ab_s.at[step], ab_r.at[step], (chip_dev(step), y))
+        ab[step].start()
+
+    first_tile, tiles = n // 128, grp // 128
+    middle = (first_tile + tiles) // 2
+    lax.fori_loop(first_tile, middle, code_tile, 0)
     arrived(daggg, d_s, d_r, 0)
     d_copies[4].start()
     arrived(daggg, d_s, d_r, 1)
     d_copies[5].start()
-    lax.fori_loop(steps // 2, steps, code_step, 0)
-
-    as_cnt[...] = dot(as_acc[...], jnp.ones((128, 128), BF16))
-    as_tx[:, 0:width] = as_f[own_half:, :].astype(BF16)
-    as_tx[:, width:] = split_count(as_cnt[own_half:, :])
-    aa = rcopy(as_tx, as_rx, aa_s, aa_r, (other, y))
-    aa.start()
+    lax.fori_loop(middle, tiles, code_tile, 0)
 
     for step in steps_out:
         wb[step].wait_recv()
@@ -379,17 +392,6 @@
     for at, (peer, slot) in enumerate(((y_right, 3), (y_left, 1), (y_far, 2))):
         wc.append(rcopy(wgc.at[0], wgc.at[slot], wc_s.at[at], wc_r.at[at], (w, peer)))
         wc[-1].start()
-
-    aa.wait_recv()
-    as_f[0:own_half, :] += as_rx[:, 0:width].astype(F32)
-    as_cnt[0:own_half, :] += join_count(as_rx[:, width:])
-    ab = {}
-    for step in steps_out:
-        rows = pl.ds(step * shard, shard)
-        asb_tx[step, :, 0:width] = as_f[rows, :].astype(BF16)
-        asb_tx[step, :, width:] = split_count(as_cnt[rows, :])
-        ab[step] = rcopy(asb_tx.at[step], asb_rx.at[step], ab_s.at[step], ab_r.at[step], (chip_dev(step), y))
-        ab[step].start()
 
     arrived(daggg, d_s, d_r, 2)
     arrived(daggg, d_s, d_r, 3)

time: 45.6 us -> 42.9 us (0.941)
  Pallas kernels: 44.8 us -> 42.1 us
    pallas_call x1, Pallas kernels: 43.8 us -> 41.1 us  [on_device(): pl.pallas_call(functools.partial(kernel, wide, narrow, shard), out_shape=...]
where the time goes in v6:
time: 42.9 us; the launch traced here: 42.8 us
  Pallas kernels  42.1 us (98%)
  between operations  0.64 us (1%)
    pallas_call x1, Pallas kernels, on_device(): pl.pallas_call(functools.partial(kernel, wide, narrow, shard), out_shape=...  41.1 us
    pallas_call x1, Pallas kernels, on_device(): pl.pallas_call(functools.partial(copy_kernel, len(shapes)), out_shape=sha...  1.03 us

profile of v6, /device:TPU:1, one launch (start us, length us, event | category | flops | bytes accessed | tf_op | source)
XLA Modules:
  0.0 42.8 jit_solution(190785769769719136)
XLA Ops:
  0.6 41.1 %shard_map.136 = (bf16[512,256]{1,0:T(8,128)(2,1)S(1)}, bf16[512,256]{1,0:T(8,128)(2,1)S(1)}, f32[256,256]{1,0:T(8,128)S(1)}, f32[256,256]{1,0:T(8,128)S(1)}, f3...) custom-call(bf16[512,256]{1,0:T(8,128)(2,1)} %feat_hbm.1, s32[8,512]{1,0:T(8,128)} %bitcast.5, s32[16,512]{1,0:T(8,128)} %bitcast.4, ...), custom_call_target="tpu_custom_call" | custom-call | tf_op jit(solution)/shard_map/pallas_call | solution.py:580
  41.7 1.0 %shard_map.137 = (bf16[512,256]{1,0:T(8,128)(2,1)}, bf16[512,256]{1,0:T(8,128)(2,1)}, f32[256,256]{1,0:T(8,128)}, f32[256,256]{1,0:T(8,128)}, f32[32,256]{1,0:T(8,128)}, /*index=5*/f32[32,256]{1,0:T(8,128)}) custom-call(bf16[512,256]{1,0:T(8,128)(2,1)S(1)} %get-tuple-element.12.refs_0_, bf16[512,256]{1,0:T(8,128)(2,1)S(1)} %get-tuple-element.13.refs_1_, ...), custom_call_target="tpu_custom_call" | custom-call | tf_op jit(solution)/shard_map/pallas_call | solution.py:590

commit v7 on v6

--- a/solution.py
+++ b/solution.py
@@ -57,11 +57,11 @@
     feat_hbm, nb_hbm, code_hbm, assign_hbm, cot_hbm, sums_hbm, counts_hbm, ws_hbm, wn_hbm,
     out, fgrad, sgrad, ngrad, newcb, cgrad,
     cot, sums, counts, ws, wn,
-    codebook, featg, daggg, idx_own, idxg, tab_far, tab_near, tab_code, tab_ret, tab_asn,
+    codebook, featg, daggg, idx_own, idxg, asg, tab_far, tab_near, tab_code, tab_ret, tab_asn,
     hi_f, val_f, hi_n, val_n, hi_t, val_t, hi_r, val_r, row_a, asn_hi, asn_lo, far, near, hid, dz_all, taken, acc,
     wg_f, wg_tx, wg_rx, wgb_tx, wgb_rx, wgc, wgd, as_f, as_cnt, as_acc, as_tx, as_rx, asb_tx, asb_rx,
     cg_tx, cg_rx, cgb_tx, cgb_rx, cnt_col,
-    in_sem, f_s, f_r, d_s, d_r, i_s, i_r, wa_s, wa_r, wb_s, wb_r, wc_s, wc_r, wd_s, wd_r, we_s, we_r,
+    in_sem, f_s, f_r, d_s, d_r, i_s, i_r, g_s, g_r, wa_s, wa_r, wb_s, wb_r, wc_s, wc_r, wd_s, wd_r, we_s, we_r,
     aa_s, aa_r, ab_s, ab_r, ca_s, ca_r, cb_s, cb_r,
 ):
     n = cot.shape[0]
@@ -111,7 +111,7 @@
                 (feat_hbm, feat),
                 (nb_hbm, idx_own.at[pl.ds(0, 8), :]),
                 (code_hbm, idx_own.at[pl.ds(8, 16), :]),
-                (assign_hbm, idx_own.at[pl.ds(24, 1), :]),
+                (assign_hbm, asg.at[0]),
                 (counts_hbm, counts),
                 (sums_hbm, sums),
                 (ws_hbm, ws),
@@ -161,6 +161,12 @@
     f_copies = gather_copies(featg, f_s, f_r)
     for at in range(4):
         f_copies[at].start()
+    g_copies = [
+        rcopy(asg.at[0], asg.at[slot], g_s.at[at], g_r.at[at], (w, peer))
+        for at, (peer, slot) in enumerate(((y_right, 3), (y_left, 1), (y_far, 2)))
+    ]
+    for copy in g_copies:
+        copy.start()
     idxg[0] = idx_own[...].astype(jnp.int16)
     i_copies = [
         rcopy(idxg.at[0], idxg.at[slot], i_s.at[at], i_r.at[at], (w, peer))
@@ -218,8 +224,6 @@
     f_copies[4].start()
     arrived(featg, f_s, f_r, 1)
     f_copies[5].start()
-    for copy in i_copies:
-        copy.start()
     near_tiles = (n // 128) * (near_spots // 128)
     step_codes = codes // near_tiles
 
@@ -239,6 +243,48 @@
     hid[...] = dot(feat[...], ws[...])
     taken[:, 0:width] = feat[...]
     near[...] = dot_tn(tab_near[0:n, :], feat[...])
+    for copy in g_copies:
+        copy.wait_recv()
+    shard_bits = shard.bit_length() - 1
+    narrow_bits = narrow.bit_length() - 1
+    mine_spots = mine // 8
+    mine_bits = mine_spots.bit_length() - 1
+    ret_spots = n // 8
+    ret_bits = ret_spots.bit_length() - 1
+
+    def place(k):
+        kw = k >> (shard_bits + narrow_bits)
+        kc = kw >> 1
+        step = ((((kc >> (x_chips.bit_length() - 1)) - chip_z) & (z_chips - 1)) * x_chips) | ((kc - chip_x) & (x_chips - 1))
+        row = ((((kw & 1) ^ core) * chips + step) << shard_bits) | (k & (shard - 1))
+        return row, ((k >> shard_bits) & (narrow - 1)) == y
+
+    for slot in range(narrow):
+        row, hit = place(asg[slot])
+        row_a[:, slot * n : slot * n + n] = jnp.where(hit, row, -1)
+
+    all_rows = row_a[...]
+    asn_hi[...] = jnp.where(lax.broadcasted_iota(I32, asn_hi.shape, 0) == (all_rows >> 4), 1.0, 0.0)
+    asn_lo[...] = jnp.where(lax.broadcasted_iota(I32, (16, grp), 0) == (all_rows & 15), 1.0, 0.0).astype(BF16)
+
+    def asn_part(group, carry):
+        totals = [None] * 8
+        for tile in range(grp // 128):
+            lanes = slice(tile * 128, tile * 128 + 128)
+            fits = asn_hi[pl.ds(pl.multiple_of(group * 8, 8), 8), lanes]
+            low = asn_lo[:, lanes]
+            for part in range(8):
+                hit = jnp.broadcast_to(fits[part : part + 1, :], (16, 128)).astype(BF16) * low
+                tab_asn[pl.ds(pl.multiple_of(group * 128 + part * 16, 16), 16), lanes] = hit
+                totals[part] = hit if tile == 0 else totals[part] + hit
+        for part in range(8):
+            as_acc[pl.ds(pl.multiple_of(group * 128 + part * 16, 16), 16), :] = totals[part]
+        return carry
+
+    lax.fori_loop(0, mine // 128, asn_part, 0)
+
+    for copy in i_copies:
+        copy.start()
     arrived(featg, f_s, f_r, 2)
     near[...] += dot_tn(tab_near[3 * n : 4 * n, :], featg[3 * n : 4 * n, :])
     arrived(featg, f_s, f_r, 3)
@@ -269,22 +315,56 @@
     wa = rcopy(wg_tx, wg_rx, wa_s, wa_r, (other, y))
     wa.start()
 
+    def split_count(count):
+        big = jnp.floor(count * (1.0 / 256)) * 256.0
+        lane = lax.broadcasted_iota(I32, count.shape, 1)
+        return jnp.where(lane < 64, big, count - big).astype(BF16)
+
+    def join_count(pair):
+        pair = pair.astype(F32)
+        return pair + pltpu.roll(pair, 64, 1)
+
+    def assigned(first):
+        rows = pl.ds(first, own_half)
+        as_f[rows, :] = dot(tab_asn[rows, :], featg[...])
+        as_cnt[rows, :] = dot(as_acc[rows, :], jnp.ones((128, 128), BF16))
+
+    assigned(own_half)
+    as_tx[:, 0:width] = as_f[own_half:, :].astype(BF16)
+    as_tx[:, width:] = split_count(as_cnt[own_half:, :])
+    aa = rcopy(as_tx, as_rx, aa_s, aa_r, (other, y))
+    aa.start()
+
+    wa.wait_recv()
+    wg_own = wg_f[core] + wg_rx[...].astype(F32)
+    wg_f[core] = wg_own
+    wgb_tx[...] = wg_own.astype(BF16)
+    part_rows = wrows // chips
+
+    def wg_rows(at):
+        return pl.ds(pl.multiple_of(at * part_rows, part_rows), part_rows)
+
+    wb = {}
+    for step in steps_out:
+        wb[step] = rcopy(
+            wgb_tx.at[wg_rows(chip_at(step)), :], wgb_rx.at[step], wb_s.at[step], wb_r.at[step], (chip_dev(step), y)
+        )
+        wb[step].start()
+    assigned(0)
+
+    aa.wait_recv()
+    as_f[0:own_half, :] += as_rx[:, 0:width].astype(F32)
+    as_cnt[0:own_half, :] += join_count(as_rx[:, width:])
+    ab = {}
+    for step in steps_out:
+        rows = pl.ds(step * shard, shard)
+        asb_tx[step, :, 0:width] = as_f[rows, :].astype(BF16)
+        asb_tx[step, :, width:] = split_count(as_cnt[rows, :])
+        ab[step] = rcopy(asb_tx.at[step], asb_rx.at[step], ab_s.at[step], ab_r.at[step], (chip_dev(step), y))
+        ab[step].start()
+
     for at in range(3):
         i_copies[at].wait_recv()
-    shard_bits = shard.bit_length() - 1
-    narrow_bits = narrow.bit_length() - 1
-    mine_spots = mine // 8
-    mine_bits = mine_spots.bit_length() - 1
-    ret_spots = n // 8
-    ret_bits = ret_spots.bit_length() - 1
-
-    def place(k):
-        kw = k >> (shard_bits + narrow_bits)
-        kc = kw >> 1
-        step = ((((kc >> (x_chips.bit_length() - 1)) - chip_z) & (z_chips - 1)) * x_chips) | ((kc - chip_x) & (x_chips - 1))
-        row = ((((kw & 1) ^ core) * chips + step) << shard_bits) | (k & (shard - 1))
-        return row, ((k >> shard_bits) & (narrow - 1)) == y
-
     for slot in range(narrow):
         lanes = pl.ds(slot * n, n)
         block = idxg[slot].astype(I32)
@@ -295,26 +375,6 @@
         row, hit = place(block[8:24, :])
         hi_t[:, lanes] = row & (mine_spots - 1)
         val_t[:, lanes] = jnp.where(hit, jnp.int32(1) << ((row >> mine_bits) * 4), 0)
-        row, hit = place(block[24:32, :])
-        row_a[:, lanes] = jnp.where(hit, row, -1)
-
-    all_rows = row_a[0:1, :]
-    asn_hi[...] = jnp.where(lax.broadcasted_iota(I32, asn_hi.shape, 0) == (all_rows >> 4), 1.0, 0.0)
-    asn_lo[...] = jnp.where(lax.broadcasted_iota(I32, (16, grp), 0) == (all_rows & 15), 1.0, 0.0).astype(BF16)
-
-    def asn_part(group, carry):
-        totals = [None] * 8
-        for tile in range(grp // 128):
-            lanes = slice(tile * 128, tile * 128 + 128)
-            fits = asn_hi[pl.ds(pl.multiple_of(group * 8, 8), 8), lanes]
-            low = asn_lo[:, lanes]
-            for part in range(8):
-                hit = jnp.broadcast_to(fits[part : part + 1, :], (16, 128)).astype(BF16) * low
-                tab_asn[pl.ds(pl.multiple_of(group * 128 + part * 16, 16), 16), lanes] = hit
-                totals[part] = hit if tile == 0 else totals[part] + hit
-        for part in range(8):
-            as_acc[pl.ds(pl.multiple_of(group * 128 + part * 16, 16), 16), :] = totals[part]
-        return carry
 
     def code_tile(tile, carry):
         table(tab_code, hi_t, val_t, mine_spots, tile * 128, 0)
@@ -323,55 +383,6 @@
     def ret_tile(tile, carry):
         table(tab_ret, hi_r, val_r, ret_spots, tile * 128, 0)
         return carry
-
-    def split_count(count):
-        big = jnp.floor(count * (1.0 / 256)) * 256.0
-        lane = lax.broadcasted_iota(I32, count.shape, 1)
-        return jnp.where(lane < 64, big, count - big).astype(BF16)
-
-    def join_count(pair):
-        pair = pair.astype(F32)
-        return pair + pltpu.roll(pair, 64, 1)
-
-    def assigned(first):
-        rows = pl.ds(first, own_half)
-        lax.fori_loop(first // 128, (first + own_half) // 128, asn_part, 0)
-        as_f[rows, :] = dot(tab_asn[rows, :], featg[...])
-        as_cnt[rows, :] = dot(as_acc[rows, :], jnp.ones((128, 128), BF16))
-
-    assigned(own_half)
-    as_tx[:, 0:width] = as_f[own_half:, :].astype(BF16)
-    as_tx[:, width:] = split_count(as_cnt[own_half:, :])
-    aa = rcopy(as_tx, as_rx, aa_s, aa_r, (other, y))
-    aa.start()
-
-    wa.wait_recv()
-    wg_own = wg_f[core] + wg_rx[...].astype(F32)
-    wg_f[core] = wg_own
-    wgb_tx[...] = wg_own.astype(BF16)
-    part_rows = wrows // chips
-
-    def wg_rows(at):
-        return pl.ds(pl.multiple_of(at * part_rows, part_rows), part_rows)
-
-    wb = {}
-    for step in steps_out:
-        wb[step] = rcopy(
-            wgb_tx.at[wg_rows(chip_at(step)), :], wgb_rx.at[step], wb_s.at[step], wb_r.at[step], (chip_dev(step), y)
-        )
-        wb[step].start()
-    assigned(0)
-
-    aa.wait_recv()
-    as_f[0:own_half, :] += as_rx[:, 0:width].astype(F32)
-    as_cnt[0:own_half, :] += join_count(as_rx[:, width:])
-    ab = {}
-    for step in steps_out:
-        rows = pl.ds(step * shard, shard)
-        asb_tx[step, :, 0:width] = as_f[rows, :].astype(BF16)
-        asb_tx[step, :, width:] = split_count(as_cnt[rows, :])
-        ab[step] = rcopy(asb_tx.at[step], asb_rx.at[step], ab_s.at[step], ab_r.at[step], (chip_dev(step), y))
-        ab[step].start()
 
     first_tile, tiles = n // 128, grp // 128
     middle = (first_tile + tiles) // 2
@@ -479,7 +490,7 @@
         own = own + cgb_rx[step].astype(F32)
     cgrad[...] = own
 
-    for copy in (*f_copies, *d_copies, *i_copies, wa, aa, *ca.values(), *wc, we):
+    for copy in (*f_copies, *d_copies, *i_copies, *g_copies, wa, aa, *ca.values(), *wc, we):
         copy.wait_send()
     for step in steps_out:
         for copies in (wb, ab, wd, cb):
@@ -518,6 +529,7 @@
         pltpu.VMEM((grp, width), BF16),
         pltpu.VMEM((IDX_ROWS, n), I32),
         pltpu.VMEM((narrow, IDX_ROWS, n), jnp.int16),
+        pltpu.VMEM((narrow, 1, n), I32),
         pltpu.VMEM((codes, n), BF16),
         pltpu.VMEM((grp, n), BF16),
         pltpu.VMEM((mine, grp), BF16),
@@ -531,7 +543,7 @@
         pltpu.VMEM((16, grp), I32),
         pltpu.VMEM((8, grp), I32),
         pltpu.VMEM((8, grp), I32),
-        pltpu.VMEM((8, grp), I32),
+        pltpu.VMEM((1, grp), I32),
         pltpu.VMEM((mine // 16, grp), F32),
         pltpu.VMEM((16, grp), BF16),
         pltpu.VMEM((n, width), F32),
@@ -560,7 +572,7 @@
         pltpu.VMEM((chips, shard, width), BF16),
         pltpu.VMEM((128, 128), F32),
         dma((9,)),
-        dma((6,)), dma((6,)), dma((6,)), dma((6,)), dma((3,)), dma((3,)),
+        dma((6,)), dma((6,)), dma((6,)), dma((6,)), dma((3,)), dma((3,)), dma((3,)), dma((3,)),
         dma, dma, dma((chips,)), dma((chips,)), dma((3,)), dma((3,)), dma((chips,)), dma((chips,)), dma, dma,
         dma, dma, dma((chips,)), dma((chips,)), dma((2,)), dma((2,)), dma((chips,)), dma((chips,)),
     ]

time: 42.9 us -> 42.3 us (0.986)
  Pallas kernels: 42.1 us -> 41.6 us
    pallas_call x1, Pallas kernels: 41.1 us -> 40.5 us  [on_device(): pl.pallas_call(functools.partial(kernel, wide, narrow, shard), out_shape=...]
where the time goes in v7:
time: 42.3 us; the launch traced here: 42.2 us
  Pallas kernels  41.6 us (98%)
  between operations  0.64 us (2%)
    pallas_call x1, Pallas kernels, on_device(): pl.pallas_call(functools.partial(kernel, wide, narrow, shard), out_shape=...  40.5 us
    pallas_call x1, Pallas kernels, on_device(): pl.pallas_call(functools.partial(copy_kernel, len(shapes)), out_shape=sha...  1.03 us

profile of v7, /device:TPU:1, one launch (start us, length us, event | category | flops | bytes accessed | tf_op | source)
XLA Modules:
  0.0 42.2 jit_solution(17684854553978950998)
XLA Ops:
  0.6 40.5 %shard_map.136 = (bf16[512,256]{1,0:T(8,128)(2,1)S(1)}, bf16[512,256]{1,0:T(8,128)(2,1)S(1)}, f32[256,256]{1,0:T(8,128)S(1)}, f32[256,256]{1,0:T(8,128)S(1)}, f3...) custom-call(bf16[512,256]{1,0:T(8,128)(2,1)} %feat_hbm.1, s32[8,512]{1,0:T(8,128)} %bitcast.5, s32[16,512]{1,0:T(8,128)} %bitcast.4, ...), custom_call_target="tpu_custom_call" | custom-call | tf_op jit(solution)/shard_map/pallas_call | solution.py:592
  41.2 1.0 %shard_map.137 = (bf16[512,256]{1,0:T(8,128)(2,1)}, bf16[512,256]{1,0:T(8,128)(2,1)}, f32[256,256]{1,0:T(8,128)}, f32[256,256]{1,0:T(8,128)}, f32[32,256]{1,0:T(8,128)}, /*index=5*/f32[32,256]{1,0:T(8,128)}) custom-call(bf16[512,256]{1,0:T(8,128)(2,1)S(1)} %get-tuple-element.12.refs_0_, bf16[512,256]{1,0:T(8,128)(2,1)S(1)} %get-tuple-element.13.refs_1_, ...), custom_call_target="tpu_custom_call" | custom-call | tf_op jit(solution)/shard_map/pallas_call | solution.py:602

commit v8 on v7

--- a/solution.py
+++ b/solution.py
@@ -139,6 +139,9 @@
     def high(slot):
         return pl.ds(slot * n + half, half)
 
+    def quarter(slot, at):
+        return pl.ds(slot * n + at * (half // 2), half // 2)
+
     def gather_copies(buf, ssem, rsem):
         right, left = (w, y_right), (w, y_left)
 
@@ -146,20 +149,27 @@
             return rcopy(buf.at[src, :], buf.at[dst, :], ssem.at[at], rsem.at[at], dev)
 
         return (
-            make(low(0), low(3), 0, right),
-            make(high(0), high(1), 1, left),
+            make(quarter(0, 0), quarter(3, 0), 0, right),
+            make(quarter(0, 2), quarter(1, 2), 1, left),
             make(high(0), high(3), 2, right),
             make(low(0), low(1), 3, left),
-            make(low(3), low(2), 4, right),
-            make(high(1), high(2), 5, left),
+            make(quarter(3, 0), quarter(2, 0), 4, right),
+            make(quarter(1, 2), quarter(2, 2), 5, left),
+            make(quarter(0, 1), quarter(3, 1), 6, right),
+            make(quarter(0, 3), quarter(1, 3), 7, left),
+            make(quarter(3, 1), quarter(2, 1), 8, right),
+            make(quarter(1, 3), quarter(2, 3), 9, left),
         )
 
     def arrived(buf, ssem, rsem, at):
-        region = (low(3), high(1), high(3), low(1), low(2), high(2))[at]
+        region = (
+            quarter(3, 0), quarter(1, 2), high(3), low(1), quarter(2, 0), quarter(2, 2),
+            quarter(3, 1), quarter(1, 3), quarter(2, 1), quarter(2, 3),
+        )[at]
         rcopy(buf.at[region, :], buf.at[region, :], ssem.at[at], rsem.at[at], (w, y_right)).wait_recv()
 
     f_copies = gather_copies(featg, f_s, f_r)
-    for at in range(4):
+    for at in (0, 1, 6, 7, 2, 3):
         f_copies[at].start()
     g_copies = [
         rcopy(asg.at[0], asg.at[slot], g_s.at[at], g_r.at[at], (w, peer))
@@ -233,7 +243,12 @@
         far[...] += dot_tn(tab_far[rows, :], codebook[rows, :])
         return carry
 
-    lax.fori_loop(0, near_tiles, near_step, 0)
+    lax.fori_loop(0, near_tiles // 4, near_step, 0)
+    arrived(featg, f_s, f_r, 6)
+    f_copies[8].start()
+    arrived(featg, f_s, f_r, 7)
+    f_copies[9].start()
+    lax.fori_loop(near_tiles // 4, near_tiles, near_step, 0)
     for kw in range(wide):
         kc = kw // 2
         step = ((kc // x_chips + z_chips - chip_z) % z_chips) * x_chips + (kc % x_chips + x_chips - chip_x) % x_chips
@@ -289,8 +304,8 @@
     near[...] += dot_tn(tab_near[3 * n : 4 * n, :], featg[3 * n : 4 * n, :])
     arrived(featg, f_s, f_r, 3)
     near[...] += dot_tn(tab_near[n : 2 * n, :], featg[n : 2 * n, :])
-    arrived(featg, f_s, f_r, 4)
-    arrived(featg, f_s, f_r, 5)
+    for at in (4, 5, 8, 9):
+        arrived(featg, f_s, f_r, at)
 
     d_copies = gather_copies(daggg, d_s, d_r)
     for at in range(2):
@@ -304,8 +319,8 @@
         dz = (cot[rows, :].astype(F32) * s * (1.0 + z * (1.0 - s))).astype(BF16)
         dz_all[rows, :] = dz
         daggg[rows, :] = dot_nt(dz, wn[...]).astype(BF16)
-        d_copies[(0, 1)[at]].start()
-        d_copies[(3, 2)[at]].start()
+        for part in ((0, 6, 3), (1, 7, 2))[at]:
+            d_copies[part].start()
 
     wrows = ws.shape[0]
     local = dot_tn(taken[...], dz_all[...])
@@ -329,27 +344,27 @@
         as_f[rows, :] = dot(tab_asn[rows, :], featg[...])
         as_cnt[rows, :] = dot(as_acc[rows, :], jnp.ones((128, 128), BF16))
 
+    wa.wait_recv()
+    wg_own = wg_f[core] + wg_rx[...].astype(F32)
+    wg_f[core] = wg_own
+    wgb_tx[...] = wg_own.astype(BF16)
+    part_rows = wrows // chips
+
+    def wg_rows(at):
+        return pl.ds(pl.multiple_of(at * part_rows, part_rows), part_rows)
+
+    wb = {}
+    for step in steps_out:
+        wb[step] = rcopy(
+            wgb_tx.at[wg_rows(chip_at(step)), :], wgb_rx.at[step], wb_s.at[step], wb_r.at[step], (chip_dev(step), y)
+        )
+        wb[step].start()
     assigned(own_half)
     as_tx[:, 0:width] = as_f[own_half:, :].astype(BF16)
     as_tx[:, width:] = split_count(as_cnt[own_half:, :])
     aa = rcopy(as_tx, as_rx, aa_s, aa_r, (other, y))
     aa.start()
 
-    wa.wait_recv()
-    wg_own = wg_f[core] + wg_rx[...].astype(F32)
-    wg_f[core] = wg_own
-    wgb_tx[...] = wg_own.astype(BF16)
-    part_rows = wrows // chips
-
-    def wg_rows(at):
-        return pl.ds(pl.multiple_of(at * part_rows, part_rows), part_rows)
-
-    wb = {}
-    for step in steps_out:
-        wb[step] = rcopy(
-            wgb_tx.at[wg_rows(chip_at(step)), :], wgb_rx.at[step], wb_s.at[step], wb_r.at[step], (chip_dev(step), y)
-        )
-        wb[step].start()
     assigned(0)
 
     aa.wait_recv()
@@ -386,12 +401,17 @@
 
     first_tile, tiles = n // 128, grp // 128
     middle = (first_tile + tiles) // 2
-    lax.fori_loop(first_tile, middle, code_tile, 0)
+    lax.fori_loop(first_tile, middle - 1, code_tile, 0)
     arrived(daggg, d_s, d_r, 0)
     d_copies[4].start()
     arrived(daggg, d_s, d_r, 1)
     d_copies[5].start()
-    lax.fori_loop(middle, tiles, code_tile, 0)
+    lax.fori_loop(middle - 1, middle + 1, code_tile, 0)
+    arrived(daggg, d_s, d_r, 6)
+    d_copies[8].start()
+    arrived(daggg, d_s, d_r, 7)
+    d_copies[9].start()
+    lax.fori_loop(middle + 1, tiles, code_tile, 0)
 
     for step in steps_out:
         wb[step].wait_recv()
@@ -407,8 +427,8 @@
     arrived(daggg, d_s, d_r, 2)
     arrived(daggg, d_s, d_r, 3)
     acc[...] = dot(tab_code[:, 0 : 2 * n], daggg[0 : 2 * n, :]) + dot(tab_code[:, 3 * n :], daggg[3 * n :, :])
-    arrived(daggg, d_s, d_r, 4)
-    arrived(daggg, d_s, d_r, 5)
+    for at in (4, 5, 8, 9):
+        arrived(daggg, d_s, d_r, at)
     last = daggg[2 * n : 3 * n, :]
     block = own_half // 2
 
@@ -572,7 +592,7 @@
         pltpu.VMEM((chips, shard, width), BF16),
         pltpu.VMEM((128, 128), F32),
         dma((9,)),
-        dma((6,)), dma((6,)), dma((6,)), dma((6,)), dma((3,)), dma((3,)), dma((3,)), dma((3,)),
+        dma((10,)), dma((10,)), dma((10,)), dma((10,)), dma((3,)), dma((3,)), dma((3,)), dma((3,)),
         dma, dma, dma((chips,)), dma((chips,)), dma((3,)), dma((3,)), dma((chips,)), dma((chips,)), dma, dma,
         dma, dma, dma((chips,)), dma((chips,)), dma((2,)), dma((2,)), dma((chips,)), dma((chips,)),
     ]

time: 42.3 us -> 42.9 us (1.014)
  Pallas kernels: 41.6 us -> 42.1 us
    pallas_call x1, Pallas kernels: 40.5 us -> 41.1 us  [on_device(): pl.pallas_call(functools.partial(kernel, wide, narrow, shard), out_shape=...]
where the time goes in v8:
time: 42.9 us; the launch traced here: 42.8 us
  Pallas kernels  42.1 us (98%)
  between operations  0.64 us (1%)
    pallas_call x1, Pallas kernels, on_device(): pl.pallas_call(functools.partial(kernel, wide, narrow, shard), out_shape=...  41.1 us
    pallas_call x1, Pallas kernels, on_device(): pl.pallas_call(functools.partial(copy_kernel, len(shapes)), out_shape=sha...  1.03 us

profile of v8, /device:TPU:1, one launch (start us, length us, event | category | flops | bytes accessed | tf_op | source)
XLA Modules:
  0.0 42.8 jit_solution(999099790729879805)
XLA Ops:
  0.6 41.1 %shard_map.136 = (bf16[512,256]{1,0:T(8,128)(2,1)S(1)}, bf16[512,256]{1,0:T(8,128)(2,1)S(1)}, f32[256,256]{1,0:T(8,128)S(1)}, f32[256,256]{1,0:T(8,128)S(1)}, f3...) custom-call(bf16[512,256]{1,0:T(8,128)(2,1)} %feat_hbm.1, s32[8,512]{1,0:T(8,128)} %bitcast.5, s32[16,512]{1,0:T(8,128)} %bitcast.4, ...), custom_call_target="tpu_custom_call" | custom-call | tf_op jit(solution)/shard_map/pallas_call | solution.py:612
  41.7 1.0 %shard_map.137 = (bf16[512,256]{1,0:T(8,128)(2,1)}, bf16[512,256]{1,0:T(8,128)(2,1)}, f32[256,256]{1,0:T(8,128)}, f32[256,256]{1,0:T(8,128)}, f32[32,256]{1,0:T(8,128)}, /*index=5*/f32[32,256]{1,0:T(8,128)}) custom-call(bf16[512,256]{1,0:T(8,128)(2,1)S(1)} %get-tuple-element.12.refs_0_, bf16[512,256]{1,0:T(8,128)(2,1)S(1)} %get-tuple-element.13.refs_1_, ...), custom_call_target="tpu_custom_call" | custom-call | tf_op jit(solution)/shard_map/pallas_call | solution.py:622
